TPU v7x, 128 devices: a whole 4x4x4 slice. The times are simulated.
128 devices in a mesh: sec: 2 (over core), op: 64 (over z, y, x).
Axes of the slice: x: 4, y: 4, z: 4, core: 2. Of those that a mesh axis runs over, the one named last changes fastest.
Arguments:
- wavefunction: bfloat16 [24, 512, 512], P('sec'), may hold values from -6 to 6
- live_rows: int32 [24], P('sec'), may hold values from 64 to 512, as said below
- left_env: bfloat16 [128, 24, 512, 512], P('op', 'sec'), may hold values from -0.75 to 0.75
- right_env: bfloat16 [128, 24, 512, 512], P('op', 'sec'), may hold values from -0.0234375 to 0.0234375
- routes: int32 [128, 24], P('op', 'sec'), may hold values from 0 to 23, as said below
Outputs:
- sigma_blocks: bfloat16 [24, 512, 512], P('sec', 'op')
Inputs may be any that keep to these rules, and one draw needn't show every extreme that they name: `live_rows`: multiples of 64; some sector has 512. For each term, routes[t] maps the 24 sectors one to one onto the 24 sectors. Sector j stands on index j // 12 of sec. Over the 2 terms of one index of op, at most 13 blocks go from one index of sec to one index of sec, and some pair reaches 13.
All inputs are finite; a program needn't handle non-finite values.
Results may differ from a plain program's by a relative error of at most 0.0049.
Values may be sent and summed in bfloat16 or wider, within the bound.
No kernel may reach another device: no remote copies, remote signals or barrier semaphores. Data moves between devices by JAX's collectives and lax.ppermute only.
A program may use at most 192 MiB of HBM per device.

v0:
```python
import jax
import jax.numpy as jnp
from jax import lax
from jax.sharding import PartitionSpec as P


def per_device(wavefunction, live_rows, left_env, right_env, routes):
    slot_count = wavefunction.shape[0]
    block_width = wavefunction.shape[1]
    term_count = left_env.shape[0]
    groups = lax.axis_size("sec")
    capacity = term_count * slot_count // groups + 1
    item_count = term_count * slot_count
    row_index = lax.broadcasted_iota(jnp.int32, wavefunction.shape, 1)
    psi_live = jnp.where(
        row_index < live_rows[:, None, None], wavefunction, jnp.zeros_like(wavefunction)
    )
    mixed_blocks = jnp.einsum(
        "tjab,jbc->tjac", left_env, psi_live, preferred_element_type=jnp.float32
    ).astype(jnp.bfloat16)
    flat_mixed = mixed_blocks.reshape(item_count, block_width, block_width)
    destination = routes.reshape(item_count)
    target = destination // slot_count
    arrival = destination % slot_count
    term_of_item = jnp.arange(item_count, dtype=jnp.int32) // slot_count
    slot_label = term_of_item * slot_count + arrival
    onehot = (target[:, None] == jnp.arange(groups, dtype=jnp.int32)[None, :]).astype(jnp.int32)
    earlier = jnp.cumsum(onehot, axis=0) - onehot
    place_in_row = jnp.sum(earlier * onehot, axis=1)
    position = target * capacity + place_in_row
    matches = position[None, :] == jnp.arange(groups * capacity, dtype=jnp.int32)[:, None]
    filled = jnp.any(matches, axis=1)
    source = jnp.argmax(matches, axis=1)
    picked_blocks = jnp.take(flat_mixed, source, axis=0)
    outgoing = jnp.where(filled[:, None, None], picked_blocks, jnp.zeros_like(picked_blocks))
    outgoing = outgoing.reshape(groups, capacity, block_width, block_width)
    slot_tags = (
        jnp.where(filled, jnp.take(slot_label, source), -1)
        .astype(jnp.bfloat16)
        .reshape(groups, capacity)
    )
    received, tags_back = (
        lax.all_to_all(outgoing, "sec", split_axis=0, concat_axis=0, tiled=True),
        lax.all_to_all(slot_tags, "sec", split_axis=0, concat_axis=0, tiled=True),
    )
    incoming = received.reshape(groups * capacity, block_width, block_width)
    tag_int = tags_back.reshape(-1).astype(jnp.int32)
    wanted = jnp.arange(item_count, dtype=jnp.int32)
    found = jnp.argmax(tag_int[None, :] == wanted[:, None], axis=1)
    chosen = jnp.take(incoming, found, axis=0).reshape(
        term_count, slot_count, block_width, block_width
    )
    partial_sum = jnp.einsum(
        "tsab,tsbc->sac", chosen, right_env, preferred_element_type=jnp.float32
    )
    reduced = lax.psum_scatter(partial_sum, "op", scatter_dimension=1, tiled=True)
    return reduced.astype(jnp.bfloat16)


def solution(mesh):
    placed = (
        P("sec", None, None),
        P("sec"),
        P("op", "sec", None, None),
        P("op", "sec", None, None),
        P("op", "sec"),
    )
    return jax.shard_map(
        per_device, mesh=mesh, in_specs=placed, out_specs=P("sec", "op", None), check_vma=False
    )
```

profile of v0, /device:TPU:24, one launch (start us, length us, event | category | flops | bytes accessed | tf_op | source)
XLA Modules:
  0.0 354.2 jit_solution(4387111449696380921)
XLA Ops:
  6.5 0.7 broadcast_remainder_fusion
  7.2 0.7 sign_compare_fusion
  7.9 0.1 div.22
  8.0 0.1 rem.31
  8.1 0.1 ne.48
  8.2 0.1 fusion.17
  8.3 0.2 select_reduce_fusion
  8.5 0.6 iota_reduce_fusion.1
  9.1 0.1 fusion.16
  9.2 0.7 gather_fusion
  9.9 0.6 convert_element_type.45
  10.6 3.2 all-to-all-start
  13.8 0.1 broadcast_in_dim.62
  13.9 0.1 broadcast_in_dim.64
  13.9 14.0 %convert_bitcast_fusion = bf16[2,12,512,512]{2,3,0,1:T(8,128)(2,1)} fusion(bf16[2,12,512,512]{3,2,1,0:T(8,128)(2,1)} %param.7, bf16[12,512,512]{2,1,0:T(8,128)(2,1)} %param.5, s32[12]{0:T(128)} %param.6), kind=kOutput, calls=%fused_computation.8 | convolution fusion | flops 6455033856 | bytes 31457328 | tf_op jit(solution)/shard_map/tjab,jbc->tjac/dot_general | solution.py:18
  27.9 16.9 %copy.22 = bf16[2,12,512,512]{3,2,1,0:T(8,128)(2,1)} copy(bf16[2,12,512,512]{2,3,0,1:T(8,128)(2,1)} %convert_bitcast_fusion) | data formatting | bytes 25165824 | tf_op jit(solution)/shard_map/convert_element_type | solution.py:20
  44.8 11.0 %gather_fusion.1 = bf16[26,512,512]{2,1,0:T(8,128)(2,1)} fusion(bf16[24,512,512]{2,1,0:T(8,128)(2,1)} %bitcast.14, s32[1024]{0:T(1024)S(1)} %pad_clamp_fusion.1), kind=kCustom, calls=%fused_computation.1 | custom fusion | bytes 27263080 | tf_op jit(solution)/shard_map/jit(_take)/gather | solution.py:34
  55.9 12.3 %select_select_fusion = bf16[2,13,512,512]{3,2,1,0:T(8,128)(2,1)} fusion(bf16[2,13,512,512]{3,2,1,0:T(8,128)(2,1)} %bitcast.15, pred[2,13]{1,0:T(4,128)(4,1)S(1)} %broadcast_in_dim.64, pred[2,13]{1,0:T(4,128)(4,1)S(1)} %broadcast_in_dim.62), kind=kLoop, calls=%fused_computation.3 | loop fusion | flops 13631488 | bytes 27263028 | tf_op jit(solution)/shard_map/jit(_where)/select_n | solution.py:35
  68.1 0.0 all-to-all-done
  68.1 8.7 %all-to-all-start.1 = ((bf16[2,13,512,512]{3,2,1,0:T(8,128)(2,1)}), bf16[2,13,512,512]{3,2,1,0:T(8,128)(2,1)}, u32[]{:S(2)}, u32[]{:S(2)}) async-start(bf16[2,13,512,512]{3,2,1,0:T(8,128)(2,1)} %select_select_fusion), calls=%async_computation.1 | async-start | bytes 27262976 | tf_op jit(solution)/shard_map/all_to_all | solution.py:43
  76.8 0.0 reduce-scatter.2.cloned.1.call-start
  76.9 0.1 reshape.129
  77.0 0.6 iota_reduce_fusion
  77.6 0.1 broadcast_in_dim.60
  77.7 10.4 %all-to-all-done.1 = bf16[2,13,512,512]{3,2,1,0:T(8,128)(2,1)} async-done(((bf16[2,13,512,512]{3,2,1,0:T(8,128)(2,1)}), bf16[2,13,512,512]{3,2,1,0:T(8,128)(2,1)}, u32[]{:S(2)}, u32[]{:S(2)}) %all-to-all-start.1) | async-done | bytes 13631520 | tf_op jit(solution)/shard_map/all_to_all | solution.py:43
  88.1 11.0 %gather_fusion.2 = bf16[24,512,512]{2,1,0:T(8,128)(2,1)} fusion(bf16[26,512,512]{2,1,0:T(8,128)(2,1)} %bitcast.4, s32[1024]{0:T(1024)S(1)} %pad_clamp_fusion), kind=kCustom, calls=%fused_computation.2 | custom fusion | bytes 25165920 | tf_op jit(solution)/shard_map/jit(_take)/gather | solution.py:50
  99.1 16.0 %fusion.12 = f32[12,512,512]{2,1,0:T(8,128)} fusion(bf16[2,12,512,512]{3,2,1,0:T(8,128)(2,1)} %param.8, bf16[2,12,512,512]{3,2,1,0:T(8,128)(2,1)} %bitcast.16, pred[2,12]{1,0:T(4,128)(4,1)S(1)} %broadcast_in_dim.60), kind=kOutput, calls=%fused_computation.15 | convolution fusion | flops 6448742400 | bytes 37748760 | tf_op jit(solution)/shard_map/tsab,tsbc->sac/dot_general | solution.py:53
  115.1 0.0 reduce-scatter.2.cloned.1.call-update
  115.1 230.6 %reduce-scatter.2.cloned.1.call-done = f32[12,8,512]{2,1,0:T(8,128)} async-done(((f32[12,512,512]{2,1,0:T(8,128)}), f32[12,8,512]{2,1,0:T(8,128)}) %reduce-scatter.2.cloned.1.call-update) | async-done | bytes 196624 | tf_op jit(solution)/shard_map/reduce_scatter | solution.py:56
  345.8 1.6 convert_element_type.43
  (10 shorter events, 0.1 us)
Async XLA Ops:
  10.6 57.5 %all-to-all-start = ((bf16[2,1,13]{2,1,0:T(2,128)(2,1)}), bf16[2,1,13]{2,1,0:T(2,128)(2,1)S(1)}, u32[]{:S(2)}, u32[]{:S(2)}) async-start(bf16[2,1,13]{2,1,0:T(2,128)(2,1)} %convert_element_type.45), calls=%async_computation | async-start | bytes 2048 | tf_op jit(solution)/shard_map/all_to_all | solution.py:44
  68.1 20.0 %all-to-all-start.1 = ((bf16[2,13,512,512]{3,2,1,0:T(8,128)(2,1)}), bf16[2,13,512,512]{3,2,1,0:T(8,128)(2,1)}, u32[]{:S(2)}, u32[]{:S(2)}) async-start(bf16[2,13,512,512]{3,2,1,0:T(8,128)(2,1)} %select_select_fusion), calls=%async_computation.1 | async-start | bytes 27262976 | tf_op jit(solution)/shard_map/all_to_all | solution.py:43
  76.8 269.0 %reduce-scatter.2.cloned.1.call-start = ((), (), s32[]{:S(2)}) async-start(), calls=%async_computation.3 | async-start | bytes 12779520 | tf_op jit(solution)/shard_map/reduce_scatter | solution.py:56
Sparse Core Ops, SparseCore 0:
  115.3 230.4 reduce-scatter.1
where the time goes:
time: 357 us; the launch traced here: 354 us
  waiting for transfers between devices  241 us (68%)
  local copies, waits for them, and re-layouts  40.8 us (11%)
  matrix products  30 us (8%)
  other arithmetic  16.9 us (5%)
  between operations  13.5 us (4%)
  starting transfers between devices  11.9 us (3%)
    reduce_scatter x1, waiting for transfers between devices, per_device(): lax.psum_scatter(partial_sum, 'op', scatter_dimension=1, tiled=True)  231 us
    convert_element_type x1, local copies, waits for them, and re-layouts, per_device(): mixed_blocks = jnp.einsum('tjab,jbc->tjac', left_env, psi_live, preferred...  16.9 us
    dot_general x1, matrix products, per_device(): jnp.einsum('tsab,tsbc->sac', chosen, right_env, preferred_element_type=jn...  16 us
    dot_general x1, matrix products, per_device(): jnp.einsum('tjab,jbc->tjac', left_env, psi_live, preferred_element_type=j...  14 us
    select_n x1, other arithmetic, per_device(): jnp.where(filled[:, None, None], picked_blocks, jnp.zeros_like(picked_blo...  12.3 us
    gather x1, local copies, waits for them, and re-layouts, per_device(): picked_blocks = jnp.take(flat_mixed, source, axis=0)  11 us
    gather x1, local copies, waits for them, and re-layouts, per_device(): jnp.take(incoming, found, axis=0)  11 us
    all_to_all x1, waiting for transfers between devices, per_device(): lax.all_to_all(outgoing, 'sec', split_axis=0, concat_axis=0, tiled=True)  10.4 us
  transfers between devices with their start and end apart: 3, of which 2 were waited for; matrix products, arithmetic and copies ran while one was open for 16% of the time, Pallas kernels for 0%

commit v1 on v0

v1 whole, which is shorter than its diff:
```python
import functools

import jax
import jax.numpy as jnp
from jax import lax
from jax.experimental import pallas as pl
from jax.experimental.pallas import tpu as pltpu
from jax.sharding import PartitionSpec as P

BF16, F32, I32 = jnp.bfloat16, jnp.float32, jnp.int32
PARTS = 3
ORDERS = ((0, 1, 2), (1, 2, 0), (2, 0, 1))
STRIDES = (16, 4, 1)
SMEM_SPEC = pl.BlockSpec(memory_space=pltpu.SMEM)
VMEM_SPEC = pl.BlockSpec(memory_space=pltpu.VMEM)
ANY_SPEC = pl.BlockSpec(memory_space=pl.ANY)


def invert_routes(routes, inverse):
    terms, slots = routes.shape
    for t in range(terms):
        for s in range(inverse.shape[1]):
            inverse[t, s] = -1
    for t in range(terms):
        for j in range(slots):
            inverse[t, routes[t, j]] = j


def list_items(inverse, owner, first, last, slots, item_t, item_j, item_s):
    count = jnp.int32(0)
    for s in range(first, last):
        for t in range(inverse.shape[0]):
            j = inverse[t, owner * slots + s]
            item_t[count] = t
            item_j[count] = j
            item_s[count] = s
            count = count + (j >= 0).astype(I32)
    return count


def masked(psi, live):
    rows = lax.broadcasted_iota(I32, psi.shape, 0)
    return jnp.where(rows < live, psi, jnp.zeros_like(psi))


def dot(a, b):
    return jnp.dot(a, b, preferred_element_type=F32)


def export_kernel(
    routes, live, psi, left, out, inverse, item_t, item_j, item_s, psi_buf, left_buf, out_buf, in_sem, out_sem
):
    slots = psi.shape[0]
    other = 1 - lax.axis_index("sec")
    invert_routes(routes, inverse)
    count = list_items(inverse, other, 0, slots, slots, item_t, item_j, item_s)

    def loads(i):
        j = item_j[i]
        return (
            pltpu.make_async_copy(left.at[item_t[i], j], left_buf.at[i], in_sem.at[0, i]),
            pltpu.make_async_copy(psi.at[j], psi_buf.at[i], in_sem.at[1, i]),
        )

    def store(i):
        return pltpu.make_async_copy(out_buf.at[i], out.at[i], out_sem.at[i])

    @pl.loop(0, count)
    def _(i):
        for copy in loads(i):
            copy.start()

    @pl.loop(0, count)
    def _(i):
        for copy in loads(i):
            copy.wait()
        out_buf[i] = dot(left_buf[i], masked(psi_buf[i], live[item_j[i]])).astype(BF16)
        store(i).start()

    @pl.loop(0, count)
    def _(i):
        store(i).wait()


def local_kernel(
    routes, live, psi, left, right, *refs
):
    sums = refs[:PARTS]
    inverse, item_t, item_j, item_s, psi_buf, left_buf, right_buf, sem = refs[PARTS:]
    slots = psi.shape[0]
    terms = left.shape[0]
    me = lax.axis_index("sec")
    invert_routes(routes, inverse)
    count = list_items(inverse, me, 0, slots, slots, item_t, item_j, item_s)

    def loads(i):
        t, j = item_t[i], item_j[i]
        return (
            pltpu.make_async_copy(left.at[t, j], left_buf.at[i], sem.at[0, i]),
            pltpu.make_async_copy(psi.at[j], psi_buf.at[i], sem.at[1, i]),
            pltpu.make_async_copy(right.at[t, item_s[i]], right_buf.at[i], sem.at[2, i]),
        )

    @pl.loop(0, count)
    def _(i):
        for copy in loads(i):
            copy.start()

    per_part = slots // PARTS
    for p in range(PARTS):
        for k in range(per_part):
            s = me * slots + p * per_part + k
            none = inverse[0, s] < 0
            for t in range(1, terms):
                none = jnp.logical_and(none, inverse[t, s] < 0)

            @pl.when(none)
            def _():
                sums[p][k] = jnp.zeros(sums[p].shape[1:], F32)

    @pl.loop(0, count)
    def _(i):
        for copy in loads(i):
            copy.wait()
        mixed = dot(left_buf[i], masked(psi_buf[i], live[item_j[i]])).astype(BF16)
        product = dot(mixed, right_buf[i])
        s = item_s[i]
        again = jnp.logical_and(i > 0, item_s[jnp.maximum(i - 1, 0)] == s)
        for p in range(PARTS):

            @pl.when(jnp.logical_and(s >= p * per_part, s < (p + 1) * per_part))
            def _():
                k = s - p * per_part
                sums[p][k] = jnp.where(again, sums[p][k], 0.0) + product


def ring_places(c, core):
    near, far = c ^ 1, 3 - c
    return (c, jnp.where(core == 0, far, near), jnp.where(core == 0, near, far), c ^ 2)


def remote_kernel(
    part, order, routes, received, right, base, send, keep, inverse, item_t, item_j, item_s, mix_buf, right_buf, total, sem
):
    slots = right.shape[1]
    terms = right.shape[0]
    per_part = base.shape[0]
    first = part * per_part
    me = lax.axis_index("sec")
    op = lax.axis_index("op")
    invert_routes(routes, inverse)
    ahead = jnp.int32(0)
    for s in range(first):
        for t in range(terms):
            ahead = ahead + (inverse[t, me * slots + s] >= 0).astype(I32)
    count = list_items(inverse, me, first, first + per_part, slots, item_t, item_j, item_s)

    def loads(i):
        return (
            pltpu.make_async_copy(received.at[ahead + i], mix_buf.at[i], sem.at[0, i]),
            pltpu.make_async_copy(right.at[item_t[i], item_s[i]], right_buf.at[i], sem.at[1, i]),
        )

    @pl.loop(0, count)
    def _(i):
        for copy in loads(i):
            copy.start()

    for k in range(per_part):
        none = inverse[0, me * slots + first + k] < 0
        for t in range(1, terms):
            none = jnp.logical_and(none, inverse[t, me * slots + first + k] < 0)

        @pl.when(none)
        def _():
            total[k] = base[k]

    @pl.loop(0, count)
    def _(i):
        for copy in loads(i):
            copy.wait()
        s = item_s[i]
        k = s - first
        again = jnp.logical_and(i > 0, item_s[jnp.maximum(i - 1, 0)] == s)
        total[k] = jnp.where(again, total[k], base[k]) + dot(mix_buf[i], right_buf[i])

    place = (op // 16, (op // 4) % 4, op % 4)
    rings = [[8 * STRIDES[a] * spot for spot in ring_places(place[a], me)] for a in order]
    half = keep.shape[0]
    for n in range(2 * half):
        row = pl.multiple_of(rings[0][n // 16] + rings[1][n // 4 % 4] + rings[2][n % 4], 8)
        rows = jnp.concatenate([total[k, pl.ds(row, 8), :] for k in range(per_part)], axis=0)
        if n < half:
            keep[n] = rows
        else:
            send[n - half] = rows.astype(BF16)


def partner_lists():
    lists = []
    for stride in STRIDES:
        pair = []
        for step in range(2):
            perm = []
            for core in range(2):
                for op in range(64):
                    c = op // stride % 4
                    d = c ^ 1 if core == step else 3 - c
                    perm.append((core * 64 + op, core * 64 + op + (d - c) * stride))
            pair.append(perm)
        lists.append(pair)
    return lists


def per_device(psi, live, left, right, routes):
    slots, rows, cols = psi.shape
    terms = left.shape[0]
    items = terms * slots
    capacity = items // 2 + 1
    per_part = slots // PARTS
    part_items = terms * per_part
    lists = [
        pltpu.SMEM((terms, 2 * slots), I32),
        pltpu.SMEM((items + 1,), I32),
        pltpu.SMEM((items + 1,), I32),
        pltpu.SMEM((items + 1,), I32),
    ]
    block = (rows, cols)
    half = 32
    other_routes = lax.ppermute(routes, "sec", [(0, 1), (1, 0)])
    flops = 2 * rows * rows * cols

    outgoing = pl.pallas_call(
        export_kernel,
        out_shape=jax.ShapeDtypeStruct((capacity,) + block, BF16),
        in_specs=[SMEM_SPEC, SMEM_SPEC, ANY_SPEC, ANY_SPEC],
        out_specs=ANY_SPEC,
        scratch_shapes=lists
        + [pltpu.VMEM((capacity,) + block, BF16)] * 3
        + [pltpu.SemaphoreType.DMA((2, capacity)), pltpu.SemaphoreType.DMA((capacity,))],
        compiler_params=pltpu.CompilerParams(vmem_limit_bytes=32 << 20),
        cost_estimate=pl.CostEstimate(flops=capacity * flops, bytes_accessed=capacity * 3 << 19, transcendentals=0),
        name="export_mixed",
    )(routes, live, psi, left)
    received = lax.ppermute(outgoing, "sec", [(0, 1), (1, 0)])

    bases = pl.pallas_call(
        local_kernel,
        out_shape=[pltpu.VMEM((per_part,) + block, F32)] * PARTS,
        in_specs=[SMEM_SPEC, SMEM_SPEC, ANY_SPEC, ANY_SPEC, ANY_SPEC],
        out_specs=[VMEM_SPEC] * PARTS,
        scratch_shapes=lists
        + [pltpu.VMEM((capacity,) + block, BF16)] * 3
        + [pltpu.SemaphoreType.DMA((3, capacity))],
        compiler_params=pltpu.CompilerParams(vmem_limit_bytes=44 << 20),
        cost_estimate=pl.CostEstimate(flops=2 * capacity * flops, bytes_accessed=capacity * 3 << 19, transcendentals=0),
        name="local_sum",
    )(routes, live, psi, left, right)

    partners = partner_lists()
    kept, coming = [], []
    for part in range(PARTS):
        send, keep = pl.pallas_call(
            functools.partial(remote_kernel, part, ORDERS[part]),
            out_shape=[
                jax.ShapeDtypeStruct((half, per_part * 8, cols), BF16),
                jax.ShapeDtypeStruct((half, per_part * 8, cols), F32),
            ],
            in_specs=[SMEM_SPEC, ANY_SPEC, ANY_SPEC, VMEM_SPEC],
            out_specs=[VMEM_SPEC, VMEM_SPEC],
            scratch_shapes=lists
            + [pltpu.VMEM((part_items,) + block, BF16)] * 2
            + [pltpu.VMEM((per_part,) + block, F32), pltpu.SemaphoreType.DMA((2, part_items))],
            compiler_params=pltpu.CompilerParams(vmem_limit_bytes=32 << 20),
            cost_estimate=pl.CostEstimate(flops=part_items * flops, bytes_accessed=part_items * 1 << 20, transcendentals=0),
            name="remote_sum",
        )(other_routes, received, right, bases[part])
        kept.append(keep)
        coming.append(lax.ppermute(send, ("sec", "op"), partners[ORDERS[part][0]][0]))

    for step in range(1, 6):
        half //= 2
        for part in range(PARTS):
            keep, come = kept[part], coming[part]
            send = (keep[half:] + come[half:].astype(F32)).astype(BF16)
            kept[part] = keep[:half] + come[:half].astype(F32)
            axis = ORDERS[part][step // 2]
            coming[part] = lax.ppermute(send, ("sec", "op"), partners[axis][step % 2])
    done = [(keep + come.astype(F32)).astype(BF16) for keep, come in zip(kept, coming)]
    return jnp.concatenate([d.reshape(per_part, 8, cols) for d in done], axis=0)


def solution(mesh):
    placed = (
        P("sec", None, None),
        P("sec"),
        P("op", "sec", None, None),
        P("op", "sec", None, None),
        P("op", "sec"),
    )
    return jax.shard_map(
        per_device, mesh=mesh, in_specs=placed, out_specs=P("sec", "op", None), check_vma=False
    )
```

time: 357 us -> 101 us (0.28)
  waiting for transfers between devices: 241 us -> 22.7 us
  Pallas kernels: 0 us -> 33.3 us
  local copies, waits for them, and re-layouts: 40.8 us -> 7.7 us
  matrix products: 30 us -> 0 us
  starting transfers between devices: 11.9 us -> 34.1 us
  other arithmetic: 16.9 us -> 2.69 us
  between operations: 13.5 us -> 0.22 us
    reduce_scatter x1 -> x0, waiting for transfers between devices: 231 us -> none  [per_device(): lax.psum_scatter(partial_sum, 'op', scatter_dimension=1, tiled=True)]
    ppermute x0 -> x20, starting transfers between devices: none -> 34.1 us  [the longest x15 28.7 us: per_device(): coming[part] = lax.ppermute(send, ('sec', 'op'), partners[axis][step % 2])]
    pallas_call x0 -> x5, Pallas kernels: none -> 33.3 us  [the longest x1 12.3 us: per_device(): pl.pallas_call(local_kernel, out_shape=[pltpu.VMEM((per_part,) + block, F...]
    dot_general x2 -> x0, matrix products: 30 us -> none  [the longest x1 16 us: per_device(): jnp.einsum('tsab,tsbc->sac', chosen, right_env, preferred_element_type=jn...]
    ppermute x0 -> x20, waiting for transfers between devices: none -> 22.7 us  [the longest x15 15 us: per_device(): coming[part] = lax.ppermute(send, ('sec', 'op'), partners[axis][step % 2])]
    gather x3 -> x0, local copies, waits for them, and re-layouts: 22.7 us -> none  [the longest x1 11 us: per_device(): picked_blocks = jnp.take(flat_mixed, source, axis=0)]
    convert_element_type x3 -> x0, local copies, waits for them, and re-layouts: 17.6 us -> none  [the longest x1 16.9 us: per_device(): mixed_blocks = jnp.einsum('tjab,jbc->tjac', left_env, psi_live, preferred...]
    select_n x3 -> x0, other arithmetic: 12.3 us -> none  [the longest x1 12.3 us: per_device(): jnp.where(filled[:, None, None], picked_blocks, jnp.zeros_like(picked_blo...]
  transfers between devices with their start and end apart: 3 -> 20, of which waited for: 2 -> 9; matrix products, arithmetic and copies ran while one was open for 16% -> 2% of each run, Pallas kernels for 0% -> 20%
where the time goes in v1:
time: 101 us
  starting transfers between devices  34.1 us (34%)
  Pallas kernels  33.3 us (33%)
  waiting for transfers between devices  22.7 us (22%)
  local copies, waits for them, and re-layouts  7.7 us (8%)
  other arithmetic  2.69 us (3%)
    ppermute x15, starting transfers between devices, per_device(): coming[part] = lax.ppermute(send, ('sec', 'op'), partners[axis][step % 2])  28.7 us
    ppermute x15, waiting for transfers between devices, per_device(): coming[part] = lax.ppermute(send, ('sec', 'op'), partners[axis][step % 2])  15 us
    pallas_call x1, Pallas kernels, per_device(): pl.pallas_call(local_kernel, out_shape=[pltpu.VMEM((per_part,) + block, F...  12.3 us
    pallas_call x3, Pallas kernels, per_device(): pl.pallas_call(functools.partial(remote_kernel, part, ORDERS[part]), out_...  12.1 us
    pallas_call x1, Pallas kernels, per_device(): pl.pallas_call(export_kernel, out_shape=jax.ShapeDtypeStruct((capacity,)...  8.87 us
    unnamed x8, local copies, waits for them, and re-layouts  7.7 us
    ppermute x3, waiting for transfers between devices, per_device(): lax.ppermute(send, ('sec', 'op'), partners[ORDERS[part][0]][0])  7.69 us
    ppermute x3, starting transfers between devices, per_device(): lax.ppermute(send, ('sec', 'op'), partners[ORDERS[part][0]][0])  4.9 us
  transfers between devices with their start and end apart: 20, of which 9 were waited for; matrix products, arithmetic and copies ran while one was open for 2% of the time, Pallas kernels for 20%

profile of v1, /device:TPU:24, one launch (start us, length us, event | category | flops | bytes accessed | tf_op | source)
XLA Modules:
  0.0 100.8 jit_solution(10747607474851846283)
XLA Ops:
  0.0 2.8 %copy-done = bf16[12,512,512]{2,1,0:T(8,128)(2,1)S(1)} copy-done((bf16[12,512,512]{2,1,0:T(8,128)(2,1)S(1)}, bf16[12,512,512]{2,1,0:T(8,128)(2,1)}, u32[]{:S(2)}) %copy-start) | copy-done | bytes 6291480
  2.8 0.7 copy-done.3
  3.4 8.9 %export_mixed.1 = bf16[13,512,512]{2,1,0:T(8,128)(2,1)} custom-call(s32[2,12]{1,0:T(2,128)} %routes.3, s32[12]{0:T(128)S(1)} %copy-done.3, bf16[12,512,512]{2,1,0:T(8,128)(2,1)S(1)} %copy-done, bf16[2,12,512,512]{3,2,1,0:T(8,128)(2,1)} %left.3), custom_call_target="tpu_custom_call" | custom-call | flops 3489660928 | bytes 20447232 | tf_op jit(solution)/shard_map/export_mixed/pallas_call | solution.py:233
  12.9 12.3 %local_sum.1 = (f32[4,512,512]{2,1,0:T(8,128)S(1)}, f32[4,512,512]{2,1,0:T(8,128)S(1)}, f32[4,512,512]{2,1,0:T(8,128)S(1)}) custom-call(s32[2,12]{1,0:T(2,128)} %routes.3, s32[12]{0:T(128)} %live.3, bf16[12,512,512]{2,1,0:T(8,128)(2,1)} %psi.3, bf16[2,12,512,512]{3,2,1,0:T(8,128)(2,1)} %left.3, bf16[2,12,512,512]{3,2,1,0:T(8,128)(2,1)} %right.7), custom_call_target="tpu_custom_call" | custom-call | flops 6979321856 | bytes 20447232 | tf_op jit(solution)/shard_map/local_sum/pallas_call | solution.py:247
  25.2 2.1 %copy-done.1 = f32[4,512,512]{2,1,0:T(8,128)} copy-done((f32[4,512,512]{2,1,0:T(8,128)}, f32[4,512,512]{2,1,0:T(8,128)S(1)}, u32[]{:S(2)}) %copy-start.1) | copy-done | bytes 4194328
  27.3 2.2 %copy-done.2 = f32[4,512,512]{2,1,0:T(8,128)S(1)} copy-done((f32[4,512,512]{2,1,0:T(8,128)S(1)}, f32[4,512,512]{2,1,0:T(8,128)}, u32[]{:S(2)}) %copy-start.2) | copy-done | bytes 4194328
  29.5 4.8 %remote_sum.3 = (bf16[32,32,512]{2,1,0:T(8,128)(2,1)S(1)}, f32[32,32,512]{2,1,0:T(8,128)S(1)}) custom-call(s32[2,12]{1,0:T(2,128)S(1)} %collective-permute-done.routes, bf16[13,512,512]{2,1,0:T(8,128)(2,1)S(1)} %collective-permute-done.1.received, bf16[2,12,512,512]{3,2,1,0:T(8,128)(2,1)} %right.7, f32[4,512,512]{2,1,0:T(8,128)S(1)} %copy-done.2), custom_call_target="tpu_custom_call" | custom-call | flops 2147483648 | bytes 8388608 | tf_op jit(solution)/shard_map/remote_sum/pallas_call | solution.py:263
  34.3 1.4 %collective-permute-start.2 = (bf16[32,32,512]{2,1,0:T(8,128)(2,1)S(1)}, bf16[32,32,512]{2,1,0:T(8,128)(2,1)S(1)}, u32[]{:S(2)}, u32[]{:S(2)}) collective-permute-start(bf16[32,32,512]{2,1,0:T(8,128)(2,1)S(1)} %get-tuple-element.16), channel_id=1, source_target_pairs={{0,16},{1,17},{2,18},{3,19},{4,20},{5,21},{6,22},{7,23},{8,24},{9,... | collective-permute-start | bytes 3145736 | tf_op jit(solution)/shard_map/ppermute | solution.py:279
  35.7 3.9 %remote_sum.4 = (bf16[32,32,512]{2,1,0:T(8,128)(2,1)S(1)}, f32[32,32,512]{2,1,0:T(8,128)S(1)}) custom-call(s32[2,12]{1,0:T(2,128)S(1)} %collective-permute-done.routes, bf16[13,512,512]{2,1,0:T(8,128)(2,1)S(1)} %collective-permute-done.1.received, bf16[2,12,512,512]{3,2,1,0:T(8,128)(2,1)} %right.7, f32[4,512,512]{2,1,0:T(8,128)S(1)} %get-tuple-element.17.base), custom_call_target="tpu_custom_call" | custom-call | flops 2147483648 | bytes 8388608 | tf_op jit(solution)/shard_map/remote_sum/pallas_call | solution.py:263
  39.6 1.4 %collective-permute-start.8 = (bf16[32,32,512]{2,1,0:T(8,128)(2,1)S(1)}, bf16[32,32,512]{2,1,0:T(8,128)(2,1)S(1)}, u32[]{:S(2)}, u32[]{:S(2)}) collective-permute-start(bf16[32,32,512]{2,1,0:T(8,128)(2,1)S(1)} %get-tuple-element.19), channel_id=1, source_target_pairs={{0,4},{1,5},{2,6},{3,7},{4,0},{5,1},{6,2},{7,3},{8,12},{9,13},{10,... | collective-permute-start | bytes 3145736 | tf_op jit(solution)/shard_map/ppermute | solution.py:279
  41.0 3.5 %remote_sum.5 = (bf16[32,32,512]{2,1,0:T(8,128)(2,1)S(1)}, f32[32,32,512]{2,1,0:T(8,128)S(1)}) custom-call(s32[2,12]{1,0:T(2,128)S(1)} %collective-permute-done.routes, bf16[13,512,512]{2,1,0:T(8,128)(2,1)S(1)} %collective-permute-done.1.received, bf16[2,12,512,512]{3,2,1,0:T(8,128)(2,1)} %right.7, f32[4,512,512]{2,1,0:T(8,128)S(1)} %get-tuple-element.20.base), custom_call_target="tpu_custom_call" | custom-call | flops 2147483648 | bytes 8388608 | tf_op jit(solution)/shard_map/remote_sum/pallas_call | solution.py:263
  44.5 2.1 %collective-permute-start.14 = (bf16[32,32,512]{2,1,0:T(8,128)(2,1)S(1)}, bf16[32,32,512]{2,1,0:T(8,128)(2,1)S(1)}, u32[]{:S(2)}, u32[]{:S(2)}) collective-permute-start(bf16[32,32,512]{2,1,0:T(8,128)(2,1)S(1)} %get-tuple-element.22), channel_id=1, source_target_pairs={{0,1},{1,0},{2,3},{3,2},{4,5},{5,4},{6,7},{7,6},{8,9},{9,8},{10,11... | collective-permute-start | bytes 3145736 | tf_op jit(solution)/shard_map/ppermute | solution.py:279
  46.6 2.6 %collective-permute-done.2 = bf16[32,32,512]{2,1,0:T(8,128)(2,1)S(1)} collective-permute-done((bf16[32,32,512]{2,1,0:T(8,128)(2,1)S(1)}, bf16[32,32,512]{2,1,0:T(8,128)(2,1)S(1)}, u32[]{:S(2)}, u32[]{:S(2)}) %collective-permute-start.2) | collective-permute-done | bytes 1048608 | tf_op jit(solution)/shard_map/ppermute | solution.py:279
  49.6 4.1 %collective-permute-start.3 = (bf16[16,32,512]{2,1,0:T(8,128)(2,1)S(1)}, bf16[16,32,512]{2,1,0:T(8,128)(2,1)S(1)}, u32[]{:S(2)}, u32[]{:S(2)}) collective-permute-start(bf16[16,32,512]{2,1,0:T(8,128)(2,1)S(1)} %get-tuple-element.23), channel_id=1, source_target_pairs={{0,48},{1,49},{2,50},{3,51},{4,52},{5,53},{6,54},{7,55},{8,56},{9,... | collective-permute-start | bytes 1572872 | tf_op jit(solution)/shard_map/ppermute | solution.py:288
  53.7 0.8 collective-permute-done.8
  55.1 4.3 %collective-permute-done.14 = bf16[32,32,512]{2,1,0:T(8,128)(2,1)S(1)} collective-permute-done((bf16[32,32,512]{2,1,0:T(8,128)(2,1)S(1)}, bf16[32,32,512]{2,1,0:T(8,128)(2,1)S(1)}, u32[]{:S(2)}, u32[]{:S(2)}) %collective-permute-start.14) | collective-permute-done | bytes 1048608 | tf_op jit(solution)/shard_map/ppermute | solution.py:279
  59.7 4.0 %collective-permute-start.15 = (bf16[16,32,512]{2,1,0:T(8,128)(2,1)S(1)}, bf16[16,32,512]{2,1,0:T(8,128)(2,1)S(1)}, u32[]{:S(2)}, u32[]{:S(2)}) collective-permute-start(bf16[16,32,512]{2,1,0:T(8,128)(2,1)S(1)} %get-tuple-element.27), channel_id=1, source_target_pairs={{0,3},{1,2},{2,1},{3,0},{4,7},{5,6},{6,5},{7,4},{8,11},{9,10},{10,... | collective-permute-start | bytes 1572872 | tf_op jit(solution)/shard_map/ppermute | solution.py:288
  64.0 1.4 %collective-permute-done.9 = bf16[16,32,512]{2,1,0:T(8,128)(2,1)S(1)} collective-permute-done((bf16[16,32,512]{2,1,0:T(8,128)(2,1)S(1)}, bf16[16,32,512]{2,1,0:T(8,128)(2,1)S(1)}, u32[]{:S(2)}, u32[]{:S(2)}) %collective-permute-start.9) | collective-permute-done | bytes 524320 | tf_op jit(solution)/shard_map/ppermute | solution.py:288
  65.6 0.9 collective-permute-start.10
  66.5 5.6 %collective-permute-done.15 = bf16[16,32,512]{2,1,0:T(8,128)(2,1)S(1)} collective-permute-done((bf16[16,32,512]{2,1,0:T(8,128)(2,1)S(1)}, bf16[16,32,512]{2,1,0:T(8,128)(2,1)S(1)}, u32[]{:S(2)}, u32[]{:S(2)}) %collective-permute-start.15) | collective-permute-done | bytes 524320 | tf_op jit(solution)/shard_map/ppermute | solution.py:288
  72.4 2.1 %collective-permute-start.5 = (bf16[4,32,512]{2,1,0:T(8,128)(2,1)S(1)}, bf16[4,32,512]{2,1,0:T(8,128)(2,1)S(1)}, u32[]{:S(2)}, u32[]{:S(2)}) collective-permute-start(bf16[4,32,512]{2,1,0:T(8,128)(2,1)S(1)} %get-tuple-element.35), channel_id=1, source_target_pairs={{0,12},{1,13},{2,14},{3,15},{4,8},{5,9},{6,10},{7,11},{8,4},{9,5},... | collective-permute-start | bytes 393224 | tf_op jit(solution)/shard_map/ppermute | solution.py:288
  74.5 2.2 %collective-permute-start.11 = (bf16[4,32,512]{2,1,0:T(8,128)(2,1)S(1)}, bf16[4,32,512]{2,1,0:T(8,128)(2,1)S(1)}, u32[]{:S(2)}, u32[]{:S(2)}) collective-permute-start(bf16[4,32,512]{2,1,0:T(8,128)(2,1)S(1)} %get-tuple-element.37), channel_id=1, source_target_pairs={{0,3},{1,2},{2,1},{3,0},{4,7},{5,6},{6,5},{7,4},{8,11},{9,10},{10,... | collective-permute-start | bytes 393224 | tf_op jit(solution)/shard_map/ppermute | solution.py:288
  76.7 2.0 %collective-permute-done.16 = bf16[8,32,512]{2,1,0:T(8,128)(2,1)S(1)} collective-permute-done((bf16[8,32,512]{2,1,0:T(8,128)(2,1)S(1)}, bf16[8,32,512]{2,1,0:T(8,128)(2,1)S(1)}, u32[]{:S(2)}, u32[]{:S(2)}) %collective-permute-start.16) | collective-permute-done | bytes 262176 | tf_op jit(solution)/shard_map/ppermute | solution.py:288
  78.7 3.4 %collective-permute-start.17 = (bf16[4,32,512]{2,1,0:T(8,128)(2,1)S(1)}, bf16[4,32,512]{2,1,0:T(8,128)(2,1)S(1)}, u32[]{:S(2)}, u32[]{:S(2)}) collective-permute-start(bf16[4,32,512]{2,1,0:T(8,128)(2,1)S(1)} %get-tuple-element.39), channel_id=1, source_target_pairs={{0,48},{1,49},{2,50},{3,51},{4,52},{5,53},{6,54},{7,55},{8,56},{9,... | collective-permute-start | bytes 393224 | tf_op jit(solution)/shard_map/ppermute | solution.py:288
  82.2 1.8 %collective-permute-start.6 = (bf16[2,32,512]{2,1,0:T(8,128)(2,1)S(1)}, bf16[2,32,512]{2,1,0:T(8,128)(2,1)S(1)}, u32[]{:S(2)}, u32[]{:S(2)}) collective-permute-start(bf16[2,32,512]{2,1,0:T(8,128)(2,1)S(1)} %get-tuple-element.41), channel_id=1, source_target_pairs={{0,1},{1,0},{2,3},{3,2},{4,5},{5,4},{6,7},{7,6},{8,9},{9,8},{10,11... | collective-permute-start | bytes 196616 | tf_op jit(solution)/shard_map/ppermute | solution.py:288
  84.3 1.0 %collective-permute-done.17 = bf16[4,32,512]{2,1,0:T(8,128)(2,1)S(1)} collective-permute-done((bf16[4,32,512]{2,1,0:T(8,128)(2,1)S(1)}, bf16[4,32,512]{2,1,0:T(8,128)(2,1)S(1)}, u32[]{:S(2)}, u32[]{:S(2)}) %collective-permute-start.17) | collective-permute-done | bytes 131104 | tf_op jit(solution)/shard_map/ppermute | solution.py:288
  85.4 3.3 %collective-permute-start.18 = (bf16[2,32,512]{2,1,0:T(8,128)(2,1)S(1)}, bf16[2,32,512]{2,1,0:T(8,128)(2,1)S(1)}, u32[]{:S(2)}, u32[]{:S(2)}) collective-permute-start(bf16[2,32,512]{2,1,0:T(8,128)(2,1)S(1)} %get-tuple-element.45), channel_id=1, source_target_pairs={{0,4},{1,5},{2,6},{3,7},{4,0},{5,1},{6,2},{7,3},{8,12},{9,13},{10,... | collective-permute-start | bytes 196616 | tf_op jit(solution)/shard_map/ppermute | solution.py:288
  88.6 2.9 %collective-permute-start.7 = (bf16[1,32,512]{2,1,0:T(8,128)(2,1)S(1)}, bf16[1,32,512]{2,1,0:T(8,128)(2,1)S(1)}, u32[]{:S(2)}, u32[]{:S(2)}) collective-permute-start(bf16[1,32,512]{2,1,0:T(8,128)(2,1)S(1)} %fusion.15), channel_id=1, source_target_pairs={{0,3},{1,2},{2,1},{3,0},{4,7},{5,6},{6,5},{7,4},{8,11},{9,10},{10,... | collective-permute-start | bytes 98312 | tf_op jit(solution)/shard_map/ppermute | solution.py:288
  91.6 3.3 %collective-permute-start.13 = (bf16[1,32,512]{2,1,0:T(8,128)(2,1)S(1)}, bf16[1,32,512]{2,1,0:T(8,128)(2,1)S(1)}, u32[]{:S(2)}, u32[]{:S(2)}) collective-permute-start(bf16[1,32,512]{2,1,0:T(8,128)(2,1)S(1)} %fusion.12), channel_id=1, source_target_pairs={{0,48},{1,49},{2,50},{3,51},{4,52},{5,53},{6,54},{7,55},{8,56},{9,... | collective-permute-start | bytes 98312 | tf_op jit(solution)/shard_map/ppermute | solution.py:288
  95.0 1.8 %collective-permute-done.13 = bf16[1,32,512]{2,1,0:T(8,128)(2,1)S(1)} collective-permute-done((bf16[1,32,512]{2,1,0:T(8,128)(2,1)S(1)}, bf16[1,32,512]{2,1,0:T(8,128)(2,1)S(1)}, u32[]{:S(2)}, u32[]{:S(2)}) %collective-permute-start.13) | collective-permute-done | bytes 32800 | tf_op jit(solution)/shard_map/ppermute | solution.py:288
  96.8 3.3 %collective-permute-done.19 = bf16[1,32,512]{2,1,0:T(8,128)(2,1)S(1)} collective-permute-done((bf16[1,32,512]{2,1,0:T(8,128)(2,1)S(1)}, bf16[1,32,512]{2,1,0:T(8,128)(2,1)S(1)}, u32[]{:S(2)}, u32[]{:S(2)}) %collective-permute-start.19) | collective-permute-done | bytes 32800 | tf_op jit(solution)/shard_map/ppermute | solution.py:288
  100.1 0.7 pad_maximum_fusion
  (40 shorter events, 3.4 us)
Async XLA Ops:
  0.0 2.8 %copy-start = (bf16[12,512,512]{2,1,0:T(8,128)(2,1)S(1)}, bf16[12,512,512]{2,1,0:T(8,128)(2,1)}, u32[]{:S(2)}) copy-start(bf16[12,512,512]{2,1,0:T(8,128)(2,1)} %psi.3) | copy-start | bytes 18874372
  2.8 0.7 copy-start.3
  12.3 15.0 %collective-permute-start.1 = (bf16[13,512,512]{2,1,0:T(8,128)(2,1)}, bf16[13,512,512]{2,1,0:T(8,128)(2,1)S(1)}, u32[]{:S(2)}, u32[]{:S(2)}) collective-permute-start(bf16[13,512,512]{2,1,0:T(8,128)(2,1)} %export_mixed.1), channel_id=1, source_target_pairs={{0,64},{64,0},{1,65},{65,1},{2,66},{66,2},{3,67},{67,3},{4,68},{68... | collective-permute-start | bytes 20447240 | tf_op jit(solution)/shard_map/ppermute | solution.py:245
  12.4 14.9 %collective-permute-start = (s32[2,12]{1,0:T(2,128)}, s32[2,12]{1,0:T(2,128)S(1)}, u32[]{:S(2)}, u32[]{:S(2)}) collective-permute-start(s32[2,12]{1,0:T(2,128)} %routes.3), channel_id=1, source_target_pairs={{0,64},{64,0},{1,65},{65,1},{2,66},{66,2},{3,67},{67,3},{4,68},{68... | collective-permute-start | bytes 296 | tf_op jit(solution)/shard_map/ppermute | solution.py:230
  25.2 2.1 %copy-start.1 = (f32[4,512,512]{2,1,0:T(8,128)}, f32[4,512,512]{2,1,0:T(8,128)S(1)}, u32[]{:S(2)}) copy-start(f32[4,512,512]{2,1,0:T(8,128)S(1)} %get-tuple-element.14.base) | copy-start | bytes 12582916
  27.3 2.2 %copy-start.2 = (f32[4,512,512]{2,1,0:T(8,128)S(1)}, f32[4,512,512]{2,1,0:T(8,128)}, u32[]{:S(2)}) copy-start(f32[4,512,512]{2,1,0:T(8,128)} %copy-done.1) | copy-start | bytes 12582916
  34.3 14.9 %collective-permute-start.2 = (bf16[32,32,512]{2,1,0:T(8,128)(2,1)S(1)}, bf16[32,32,512]{2,1,0:T(8,128)(2,1)S(1)}, u32[]{:S(2)}, u32[]{:S(2)}) collective-permute-start(bf16[32,32,512]{2,1,0:T(8,128)(2,1)S(1)} %get-tuple-element.16), channel_id=1, source_target_pairs={{0,16},{1,17},{2,18},{3,19},{4,20},{5,21},{6,22},{7,23},{8,24},{9,... | collective-permute-start | bytes 3145736 | tf_op jit(solution)/shard_map/ppermute | solution.py:279
  39.6 14.9 %collective-permute-start.8 = (bf16[32,32,512]{2,1,0:T(8,128)(2,1)S(1)}, bf16[32,32,512]{2,1,0:T(8,128)(2,1)S(1)}, u32[]{:S(2)}, u32[]{:S(2)}) collective-permute-start(bf16[32,32,512]{2,1,0:T(8,128)(2,1)S(1)} %get-tuple-element.19), channel_id=1, source_target_pairs={{0,4},{1,5},{2,6},{3,7},{4,0},{5,1},{6,2},{7,3},{8,12},{9,13},{10,... | collective-permute-start | bytes 3145736 | tf_op jit(solution)/shard_map/ppermute | solution.py:279
  44.5 14.9 %collective-permute-start.14 = (bf16[32,32,512]{2,1,0:T(8,128)(2,1)S(1)}, bf16[32,32,512]{2,1,0:T(8,128)(2,1)S(1)}, u32[]{:S(2)}, u32[]{:S(2)}) collective-permute-start(bf16[32,32,512]{2,1,0:T(8,128)(2,1)S(1)} %get-tuple-element.22), channel_id=1, source_target_pairs={{0,1},{1,0},{2,3},{3,2},{4,5},{5,4},{6,7},{7,6},{8,9},{9,8},{10,11... | collective-permute-start | bytes 3145736 | tf_op jit(solution)/shard_map/ppermute | solution.py:279
  49.6 14.2 %collective-permute-start.3 = (bf16[16,32,512]{2,1,0:T(8,128)(2,1)S(1)}, bf16[16,32,512]{2,1,0:T(8,128)(2,1)S(1)}, u32[]{:S(2)}, u32[]{:S(2)}) collective-permute-start(bf16[16,32,512]{2,1,0:T(8,128)(2,1)S(1)} %get-tuple-element.23), channel_id=1, source_target_pairs={{0,48},{1,49},{2,50},{3,51},{4,52},{5,53},{6,54},{7,55},{8,56},{9,... | collective-permute-start | bytes 1572872 | tf_op jit(solution)/shard_map/ppermute | solution.py:288
  54.9 10.5 %collective-permute-start.9 = (bf16[16,32,512]{2,1,0:T(8,128)(2,1)S(1)}, bf16[16,32,512]{2,1,0:T(8,128)(2,1)S(1)}, u32[]{:S(2)}, u32[]{:S(2)}) collective-permute-start(bf16[16,32,512]{2,1,0:T(8,128)(2,1)S(1)} %get-tuple-element.25), channel_id=1, source_target_pairs={{0,12},{1,13},{2,14},{3,15},{4,8},{5,9},{6,10},{7,11},{8,4},{9,5},... | collective-permute-start | bytes 1572872 | tf_op jit(solution)/shard_map/ppermute | solution.py:288
  59.7 12.3 %collective-permute-start.15 = (bf16[16,32,512]{2,1,0:T(8,128)(2,1)S(1)}, bf16[16,32,512]{2,1,0:T(8,128)(2,1)S(1)}, u32[]{:S(2)}, u32[]{:S(2)}) collective-permute-start(bf16[16,32,512]{2,1,0:T(8,128)(2,1)S(1)} %get-tuple-element.27), channel_id=1, source_target_pairs={{0,3},{1,2},{2,1},{3,0},{4,7},{5,6},{6,5},{7,4},{8,11},{9,10},{10,... | collective-permute-start | bytes 1572872 | tf_op jit(solution)/shard_map/ppermute | solution.py:288
  63.9 8.4 %collective-permute-start.4 = (bf16[8,32,512]{2,1,0:T(8,128)(2,1)S(1)}, bf16[8,32,512]{2,1,0:T(8,128)(2,1)S(1)}, u32[]{:S(2)}, u32[]{:S(2)}) collective-permute-start(bf16[8,32,512]{2,1,0:T(8,128)(2,1)S(1)} %get-tuple-element.29), channel_id=1, source_target_pairs={{0,4},{1,5},{2,6},{3,7},{4,0},{5,1},{6,2},{7,3},{8,12},{9,13},{10,... | collective-permute-start | bytes 786440 | tf_op jit(solution)/shard_map/ppermute | solution.py:288
  65.6 8.9 %collective-permute-start.10 = (bf16[8,32,512]{2,1,0:T(8,128)(2,1)S(1)}, bf16[8,32,512]{2,1,0:T(8,128)(2,1)S(1)}, u32[]{:S(2)}, u32[]{:S(2)}) collective-permute-start(bf16[8,32,512]{2,1,0:T(8,128)(2,1)S(1)} %get-tuple-element.31), channel_id=1, source_target_pairs={{0,1},{1,0},{2,3},{3,2},{4,5},{5,4},{6,7},{7,6},{8,9},{9,8},{10,11... | collective-permute-start | bytes 786440 | tf_op jit(solution)/shard_map/ppermute | solution.py:288
  72.2 6.5 %collective-permute-start.16 = (bf16[8,32,512]{2,1,0:T(8,128)(2,1)S(1)}, bf16[8,32,512]{2,1,0:T(8,128)(2,1)S(1)}, u32[]{:S(2)}, u32[]{:S(2)}) collective-permute-start(bf16[8,32,512]{2,1,0:T(8,128)(2,1)S(1)} %get-tuple-element.33), channel_id=1, source_target_pairs={{0,16},{1,17},{2,18},{3,19},{4,20},{5,21},{6,22},{7,23},{8,24},{9,... | collective-permute-start | bytes 786440 | tf_op jit(solution)/shard_map/ppermute | solution.py:288
  72.4 9.7 %collective-permute-start.5 = (bf16[4,32,512]{2,1,0:T(8,128)(2,1)S(1)}, bf16[4,32,512]{2,1,0:T(8,128)(2,1)S(1)}, u32[]{:S(2)}, u32[]{:S(2)}) collective-permute-start(bf16[4,32,512]{2,1,0:T(8,128)(2,1)S(1)} %get-tuple-element.35), channel_id=1, source_target_pairs={{0,12},{1,13},{2,14},{3,15},{4,8},{5,9},{6,10},{7,11},{8,4},{9,5},... | collective-permute-start | bytes 393224 | tf_op jit(solution)/shard_map/ppermute | solution.py:288
  74.5 9.4 %collective-permute-start.11 = (bf16[4,32,512]{2,1,0:T(8,128)(2,1)S(1)}, bf16[4,32,512]{2,1,0:T(8,128)(2,1)S(1)}, u32[]{:S(2)}, u32[]{:S(2)}) collective-permute-start(bf16[4,32,512]{2,1,0:T(8,128)(2,1)S(1)} %get-tuple-element.37), channel_id=1, source_target_pairs={{0,3},{1,2},{2,1},{3,0},{4,7},{5,6},{6,5},{7,4},{8,11},{9,10},{10,... | collective-permute-start | bytes 393224 | tf_op jit(solution)/shard_map/ppermute | solution.py:288
  78.7 6.6 %collective-permute-start.17 = (bf16[4,32,512]{2,1,0:T(8,128)(2,1)S(1)}, bf16[4,32,512]{2,1,0:T(8,128)(2,1)S(1)}, u32[]{:S(2)}, u32[]{:S(2)}) collective-permute-start(bf16[4,32,512]{2,1,0:T(8,128)(2,1)S(1)} %get-tuple-element.39), channel_id=1, source_target_pairs={{0,48},{1,49},{2,50},{3,51},{4,52},{5,53},{6,54},{7,55},{8,56},{9,... | collective-permute-start | bytes 393224 | tf_op jit(solution)/shard_map/ppermute | solution.py:288
  82.2 6.4 %collective-permute-start.6 = (bf16[2,32,512]{2,1,0:T(8,128)(2,1)S(1)}, bf16[2,32,512]{2,1,0:T(8,128)(2,1)S(1)}, u32[]{:S(2)}, u32[]{:S(2)}) collective-permute-start(bf16[2,32,512]{2,1,0:T(8,128)(2,1)S(1)} %get-tuple-element.41), channel_id=1, source_target_pairs={{0,1},{1,0},{2,3},{3,2},{4,5},{5,4},{6,7},{7,6},{8,9},{9,8},{10,11... | collective-permute-start | bytes 196616 | tf_op jit(solution)/shard_map/ppermute | solution.py:288
  84.0 7.6 %collective-permute-start.12 = (bf16[2,32,512]{2,1,0:T(8,128)(2,1)S(1)}, bf16[2,32,512]{2,1,0:T(8,128)(2,1)S(1)}, u32[]{:S(2)}, u32[]{:S(2)}) collective-permute-start(bf16[2,32,512]{2,1,0:T(8,128)(2,1)S(1)} %get-tuple-element.43), channel_id=1, source_target_pairs={{0,16},{1,17},{2,18},{3,19},{4,20},{5,21},{6,22},{7,23},{8,24},{9,... | collective-permute-start | bytes 196616 | tf_op jit(solution)/shard_map/ppermute | solution.py:288
  85.4 9.5 %collective-permute-start.18 = (bf16[2,32,512]{2,1,0:T(8,128)(2,1)S(1)}, bf16[2,32,512]{2,1,0:T(8,128)(2,1)S(1)}, u32[]{:S(2)}, u32[]{:S(2)}) collective-permute-start(bf16[2,32,512]{2,1,0:T(8,128)(2,1)S(1)} %get-tuple-element.45), channel_id=1, source_target_pairs={{0,4},{1,5},{2,6},{3,7},{4,0},{5,1},{6,2},{7,3},{8,12},{9,13},{10,... | collective-permute-start | bytes 196616 | tf_op jit(solution)/shard_map/ppermute | solution.py:288
  88.6 6.4 %collective-permute-start.7 = (bf16[1,32,512]{2,1,0:T(8,128)(2,1)S(1)}, bf16[1,32,512]{2,1,0:T(8,128)(2,1)S(1)}, u32[]{:S(2)}, u32[]{:S(2)}) collective-permute-start(bf16[1,32,512]{2,1,0:T(8,128)(2,1)S(1)} %fusion.15), channel_id=1, source_target_pairs={{0,3},{1,2},{2,1},{3,0},{4,7},{5,6},{6,5},{7,4},{8,11},{9,10},{10,... | collective-permute-start | bytes 98312 | tf_op jit(solution)/shard_map/ppermute | solution.py:288
  91.6 5.2 %collective-permute-start.13 = (bf16[1,32,512]{2,1,0:T(8,128)(2,1)S(1)}, bf16[1,32,512]{2,1,0:T(8,128)(2,1)S(1)}, u32[]{:S(2)}, u32[]{:S(2)}) collective-permute-start(bf16[1,32,512]{2,1,0:T(8,128)(2,1)S(1)} %fusion.12), channel_id=1, source_target_pairs={{0,48},{1,49},{2,50},{3,51},{4,52},{5,53},{6,54},{7,55},{8,56},{9,... | collective-permute-start | bytes 98312 | tf_op jit(solution)/shard_map/ppermute | solution.py:288
  94.9 5.2 %collective-permute-start.19 = (bf16[1,32,512]{2,1,0:T(8,128)(2,1)S(1)}, bf16[1,32,512]{2,1,0:T(8,128)(2,1)S(1)}, u32[]{:S(2)}, u32[]{:S(2)}) collective-permute-start(bf16[1,32,512]{2,1,0:T(8,128)(2,1)S(1)} %fusion.9), channel_id=1, source_target_pairs={{0,12},{1,13},{2,14},{3,15},{4,8},{5,9},{6,10},{7,11},{8,4},{9,5},... | collective-permute-start | bytes 98312 | tf_op jit(solution)/shard_map/ppermute | solution.py:288

commit v2 on v0

v2 whole, which is shorter than its diff:
```python
import functools

import jax
import jax.numpy as jnp
from jax import lax
from jax.experimental import pallas as pl
from jax.experimental.pallas import tpu as pltpu
from jax.sharding import PartitionSpec as P

BF16, F32, I32 = jnp.bfloat16, jnp.float32, jnp.int32
PARTS = 3
PAD = 64
LIST, EXPORT, LOCAL, HERE, SLOT, PLAN = 32, 0, 64, 128, 160, 192
ORDERS = ((0, 1, 2), (1, 2, 0), (2, 0, 1))
STRIDES = (16, 4, 1)
SMEM_SPEC = pl.BlockSpec(memory_space=pltpu.SMEM)
VMEM_SPEC = pl.BlockSpec(memory_space=pltpu.VMEM)
ANY_SPEC = pl.BlockSpec(memory_space=pl.ANY)
HBM_SPEC = pl.BlockSpec(memory_space=pltpu.HBM)


def dot(a, b):
    return jnp.dot(a, b, preferred_element_type=F32)


def cleared(psi_live, j, live):
    rows, cols = psi_live.shape[1:]

    @pl.loop(live // PAD, rows // PAD)
    def _(n):
        psi_live[j, pl.ds(pl.multiple_of(n * PAD, PAD), PAD), :] = jnp.zeros((PAD, cols), BF16)


def waited(source, target, sem):
    @pl.loop(0, target.shape[0])
    def _(i):
        pltpu.make_async_copy(source.at[0, 0], target.at[i], sem.at[i]).wait()


def first_kernel(
    routes_in, live_in, psi, left, out, psi_live, ahead, plan, routes, live, inverse, state, left_buf,
    table_sem, psi_sem, left_sem, ahead_sem
):
    terms, slots = routes.shape
    me = lax.axis_index("sec")
    tables = (
        pltpu.make_async_copy(routes_in, routes, table_sem.at[0]),
        pltpu.make_async_copy(live_in, live, table_sem.at[1]),
    )
    for copy in tables:
        copy.start()

    quarter = psi.shape[1] // 4

    def load_psi(j, q):
        piece = pl.ds(quarter * q, quarter)
        return pltpu.make_async_copy(psi.at[j, piece, :], psi_live.at[j, piece, :], psi_sem.at[j, q])

    def each_live_quarter(j, do):
        for q in range(4):
            pl.when(live[j] > quarter * q)(functools.partial(do, j, q))

    def want_psi(j):
        @pl.when(state[j] == 0)
        def _():
            each_live_quarter(j, lambda j, q: load_psi(j, q).start())
            state[j] = 1

    def have_psi(j):
        @pl.when(state[j] == 1)
        def _():
            each_live_quarter(j, lambda j, q: load_psi(j, q).wait())
            cleared(psi_live, j, live[j])
            state[j] = 2

    for j in range(slots):
        state[j] = 0
    for t in range(terms):
        for s in range(2 * slots):
            inverse[t, s] = -1
    for copy in tables:
        copy.wait()
    for t in range(terms):
        for j in range(slots):
            inverse[t, routes[t, j]] = j

    def listed(owner, at):
        count = jnp.int32(0)
        for s in range(slots):
            for t in range(terms):
                j = inverse[t, owner * slots + s]
                plan[at + count] = t
                plan[at + LIST + count] = j
                count = count + (j >= 0).astype(I32)
        for n in range(11, 13):
            plan[at + n] = jnp.where(n < count, plan[at + n], plan[at + 10])
            plan[at + LIST + n] = jnp.where(n < count, plan[at + LIST + n], plan[at + LIST + 10])

    first = out.shape[0]
    listed(1 - me, EXPORT)

    def load_left(i):
        source = left.at[plan[EXPORT + i], plan[EXPORT + LIST + i]]
        return pltpu.make_async_copy(source, left_buf.at[i], left_sem.at[i])

    @pl.loop(0, first)
    def _(i):
        want_psi(plan[EXPORT + LIST + i])
        load_left(i).start()

    @pl.loop(0, slots)
    def _(j):
        want_psi(j)

    listed(me, LOCAL)

    @pl.loop(0, ahead.shape[0])
    def _(i):
        at = EXPORT + first + i
        pltpu.make_async_copy(left.at[plan[at], plan[at + LIST]], ahead.at[i], ahead_sem.at[i]).start()

    local_count = jnp.int32(0)
    other_count = jnp.int32(0)
    for s in range(slots):
        for t in range(terms):
            here = (inverse[t, me * slots + s] >= 0).astype(I32)
            plan[HERE + terms * s + t] = here
            plan[SLOT + terms * s + t] = jnp.where(here == 1, local_count, other_count)
            local_count = local_count + here
            other_count = other_count + 1 - here
    for group in (range(first // 2), range(first // 2, first)):
        for i in group:
            have_psi(plan[EXPORT + LIST + i])
            load_left(i).wait()
        for i in group:
            out[i] = dot(left_buf[i], psi_live[plan[EXPORT + LIST + i]]).astype(BF16)
    for j in range(slots):
        have_psi(j)
    waited(left, ahead, ahead_sem)


def last_kernel(plan, psi_live, ahead, left, out, left_local, sem):
    count = out.shape[0]

    @pl.loop(0, left_local.shape[0])
    def _(i):
        at = LOCAL + i
        pltpu.make_async_copy(left.at[plan[at], plan[at + LIST]], left_local.at[i], sem.at[i]).start()

    for i in range(count):
        out[i] = dot(ahead[i], psi_live[plan[EXPORT + LIST + 13 - count + i]]).astype(BF16)
    waited(left, left_local, sem)


def load_right(right, part, target, sem):
    terms, _, rows, _ = right.shape
    per_part = target.shape[0]

    def load(k, t):
        source = right.at[t, part * per_part + k]
        return pltpu.make_async_copy(source, target.at[k, pl.ds(rows * t, rows), :], sem.at[k, t])

    @pl.loop(0, per_part)
    def _(k):
        for t in range(terms):
            load(k, t).start()

    def wait():
        @pl.loop(0, per_part)
        def _(k):
            for t in range(terms):
                load(k, t).wait()

    return wait


def local_kernel(plan, psi_live, left_local, right, out, right_part, sem):
    wait = load_right(right, 0, right_part, sem)
    for i in range(out.shape[0]):
        out[i] = dot(left_local[i], psi_live[plan[LOCAL + LIST + i]]).astype(BF16)
    wait()


def ring_places(c, core):
    near, far = c ^ 1, 3 - c
    return (c, jnp.where(core == 0, far, near), jnp.where(core == 0, near, far), c ^ 2)


def part_kernel(part, order, *refs):
    if part < PARTS - 1:
        plan, local_mixed, *received, right_part, right, send, keep, right_next, total, mixed, sem = refs
        wait = load_right(right, part + 1, right_next, sem)
    else:
        plan, local_mixed, *received, right_part, send, keep, total, mixed = refs
    per_part, rows, _ = total.shape
    terms = right_part.shape[1] // rows
    me = lax.axis_index("sec")
    op = lax.axis_index("op")
    place = (op // 16, (op // 4) % 4, op % 4)
    rings = [[8 * STRIDES[a] * spot for spot in ring_places(place[a], me)] for a in order]
    half = keep.shape[0]

    def block(s, t):
        here, slot = plan[HERE + terms * s + t], plan[SLOT + terms * s + t]
        last = received[0].shape[0] - 1
        came = received[0][jnp.minimum(slot, last)]
        if len(received) > 1:
            came = jnp.where(slot > last, received[1][jnp.clip(slot - last - 1, 0, received[1].shape[0] - 1)], came)
        return jnp.where(here == 1, local_mixed[slot], came)

    for k in range(per_part):
        s = part * per_part + k
        for t in range(terms):
            mixed[k, :, rows * t : rows * (t + 1)] = block(s, t)
        total[k] = dot(mixed[k], right_part[k])
    for pair in range(per_part // 2):
        for n in range(2 * half):
            row = pl.multiple_of(rings[0][n // 16] + rings[1][n // 4 % 4] + rings[2][n % 4], 8)
            piece = jnp.concatenate([total[2 * pair + e, pl.ds(row, 8), :] for e in range(2)], axis=0)
            if n < half:
                keep[n, pl.ds(16 * pair, 16), :] = piece
            else:
                send[n - half, pl.ds(16 * pair, 16), :] = piece.astype(BF16)
    if part < PARTS - 1:
        wait()


def partner_lists():
    lists = []
    for stride in STRIDES:
        pair = []
        for step in range(2):
            perm = []
            for core in range(2):
                for op in range(64):
                    c = op // stride % 4
                    d = c ^ 1 if core == step else 3 - c
                    perm.append((core * 64 + op, core * 64 + op + (d - c) * stride))
            pair.append(perm)
        lists.append(pair)
    return lists


def per_device(psi, live, left, right, routes):
    slots, rows, cols = psi.shape
    terms = left.shape[0]
    items = terms * slots
    capacity = items // 2 + 1
    per_part = slots // PARTS
    part_items = terms * per_part
    psi, live, left, right, routes = (
        pltpu.with_memory_space_constraint(x, pltpu.HBM) for x in (psi, live, left, right, routes)
    )
    block = (rows, cols)
    half = 32
    swap = [(0, 1), (1, 0)]
    flops = 2 * rows * rows * cols
    first, last = part_items, capacity - part_items

    def cost(dots, blocks):
        return pl.CostEstimate(flops=dots * flops, bytes_accessed=blocks * rows * cols * 2, transcendentals=0)

    def blocks(*count):
        return pltpu.VMEM(count + block, BF16)

    def params(mib):
        return pltpu.CompilerParams(vmem_limit_bytes=mib << 20)

    outgoing, psi_live, ahead, plan = pl.pallas_call(
        first_kernel,
        out_shape=[blocks(first), blocks(slots), blocks(last), pltpu.SMEM((PLAN,), I32)],
        in_specs=[HBM_SPEC] * 4,
        out_specs=[VMEM_SPEC] * 3 + [SMEM_SPEC],
        scratch_shapes=[
            pltpu.SMEM((terms, slots), I32),
            pltpu.SMEM((slots,), I32),
            pltpu.SMEM((terms, 2 * slots), I32),
            pltpu.SMEM((slots,), I32),
            blocks(first),
            pltpu.SemaphoreType.DMA((2,)),
            pltpu.SemaphoreType.DMA((slots, 4)),
            pltpu.SemaphoreType.DMA((first,)),
            pltpu.SemaphoreType.DMA((last,)),
        ],
        compiler_params=params(8),
        cost_estimate=cost(first, 2 * capacity),
        name="first_exports",
    )(routes, live, psi, left)
    received = [lax.ppermute(outgoing, "sec", swap)]

    outgoing, left_local = pl.pallas_call(
        last_kernel,
        out_shape=[blocks(last), blocks(capacity)],
        in_specs=[SMEM_SPEC, VMEM_SPEC, VMEM_SPEC, HBM_SPEC],
        out_specs=[VMEM_SPEC] * 2,
        scratch_shapes=[pltpu.SemaphoreType.DMA((capacity,))],
        compiler_params=params(4),
        cost_estimate=cost(last, capacity),
        name="last_exports",
    )(plan, psi_live, ahead, left)
    received.append(lax.ppermute(outgoing, "sec", swap))

    right_blocks = pltpu.VMEM((per_part, terms * rows, cols), BF16)
    right_sem = pltpu.SemaphoreType.DMA((per_part, terms))
    local_mixed, right_part = pl.pallas_call(
        local_kernel,
        out_shape=[blocks(capacity), right_blocks],
        in_specs=[SMEM_SPEC, VMEM_SPEC, VMEM_SPEC, HBM_SPEC],
        out_specs=[VMEM_SPEC] * 2,
        scratch_shapes=[right_sem],
        compiler_params=params(4),
        cost_estimate=cost(capacity, items),
        name="local_mixed",
    )(plan, psi_live, left_local, right)

    partners = partner_lists()
    kept, coming = [], []
    for part in range(PARTS):
        arrived = received if part else received[:1]
        ahead_of = part < PARTS - 1
        send, keep, *right_next = pl.pallas_call(
            functools.partial(part_kernel, part, ORDERS[part]),
            out_shape=[
                pltpu.VMEM((half, per_part * 8, cols), BF16),
                pltpu.VMEM((half, per_part * 8, cols), F32),
            ]
            + [right_blocks] * ahead_of,
            in_specs=[SMEM_SPEC] + [VMEM_SPEC] * (2 + len(arrived)) + [HBM_SPEC] * ahead_of,
            out_specs=[VMEM_SPEC] * (2 + ahead_of),
            scratch_shapes=[
                pltpu.VMEM((per_part,) + block, F32),
                pltpu.VMEM((per_part, rows, terms * rows), BF16),
            ]
            + [right_sem] * ahead_of,
            compiler_params=params(12),
            cost_estimate=cost(10 * part_items, part_items),
            name="part_sums",
        )(plan, local_mixed, *arrived, right_part, *[right] * ahead_of)
        right_part = right_next[0] if ahead_of else None
        kept.append(keep)
        coming.append(lax.ppermute(send, ("sec", "op"), partners[ORDERS[part][0]][0]))

    for step in range(1, 6):
        half //= 2
        for part in range(PARTS):
            keep, come = kept[part], coming[part]
            send = (keep[half:] + come[half:].astype(F32)).astype(BF16)
            kept[part] = keep[:half] + come[:half].astype(F32)
            axis = ORDERS[part][step // 2]
            coming[part] = lax.ppermute(send, ("sec", "op"), partners[axis][step % 2])
    done = [(keep + come.astype(F32)).astype(BF16) for keep, come in zip(kept, coming)]
    return jnp.concatenate([d.reshape(per_part, 8, cols) for d in done], axis=0)


def solution(mesh):
    placed = (
        P("sec", None, None),
        P("sec"),
        P("op", "sec", None, None),
        P("op", "sec", None, None),
        P("op", "sec"),
    )
    return jax.shard_map(
        per_device, mesh=mesh, in_specs=placed, out_specs=P("sec", "op", None), check_vma=False
    )
```

time: 357 us -> 80.4 us (0.23)
  waiting for transfers between devices: 241 us -> 21.1 us
  local copies, waits for them, and re-layouts: 40.8 us -> 0 us
  matrix products: 30 us -> 0 us
  starting transfers between devices: 11.9 us -> 35.1 us
  Pallas kernels: 0 us -> 21.3 us
  other arithmetic: 16.9 us -> 2.56 us
  between operations: 13.5 us -> 0.21 us
    reduce_scatter x1 -> x0, waiting for transfers between devices: 231 us -> none  [per_device(): lax.psum_scatter(partial_sum, 'op', scatter_dimension=1, tiled=True)]
    ppermute x0 -> x20, starting transfers between devices: none -> 35.1 us  [the longest x15 29.9 us: per_device(): coming[part] = lax.ppermute(send, ('sec', 'op'), partners[axis][step % 2])]
    dot_general x2 -> x0, matrix products: 30 us -> none  [the longest x1 16 us: per_device(): jnp.einsum('tsab,tsbc->sac', chosen, right_env, preferred_element_type=jn...]
    gather x3 -> x0, local copies, waits for them, and re-layouts: 22.7 us -> none  [the longest x1 11 us: per_device(): picked_blocks = jnp.take(flat_mixed, source, axis=0)]
    pallas_call x0 -> x6, Pallas kernels: none -> 21.3 us  [the longest x3 7.95 us: per_device(): pl.pallas_call(functools.partial(part_kernel, part, ORDERS[part]), out_sh...]
    ppermute x0 -> x20, waiting for transfers between devices: none -> 21.1 us  [the longest x15 12.9 us: per_device(): coming[part] = lax.ppermute(send, ('sec', 'op'), partners[axis][step % 2])]
    convert_element_type x3 -> x0, local copies, waits for them, and re-layouts: 17.6 us -> none  [the longest x1 16.9 us: per_device(): mixed_blocks = jnp.einsum('tjab,jbc->tjac', left_env, psi_live, preferred...]
    select_n x3 -> x0, other arithmetic: 12.3 us -> none  [the longest x1 12.3 us: per_device(): jnp.where(filled[:, None, None], picked_blocks, jnp.zeros_like(picked_blo...]
  transfers between devices with their start and end apart: 3 -> 20, of which waited for: 2 -> 10; matrix products, arithmetic and copies ran while one was open for 16% -> 2% of each run, Pallas kernels for 0% -> 18%
where the time goes in v2:
time: 80.4 us; the launch traced here: 80.3 us
  starting transfers between devices  35.1 us (44%)
  Pallas kernels  21.3 us (26%)
  waiting for transfers between devices  21.1 us (26%)
  other arithmetic  2.56 us (3%)
    ppermute x15, starting transfers between devices, per_device(): coming[part] = lax.ppermute(send, ('sec', 'op'), partners[axis][step % 2])  29.9 us
    ppermute x15, waiting for transfers between devices, per_device(): coming[part] = lax.ppermute(send, ('sec', 'op'), partners[axis][step % 2])  12.9 us
    ppermute x3, waiting for transfers between devices, per_device(): lax.ppermute(send, ('sec', 'op'), partners[ORDERS[part][0]][0])  8.16 us
    pallas_call x3, Pallas kernels, per_device(): pl.pallas_call(functools.partial(part_kernel, part, ORDERS[part]), out_sh...  7.95 us
    pallas_call x1, Pallas kernels, per_device(): pl.pallas_call(first_kernel, out_shape=[blocks(first), blocks(slots), blo...  6.47 us
    ppermute x3, starting transfers between devices, per_device(): lax.ppermute(send, ('sec', 'op'), partners[ORDERS[part][0]][0])  4.52 us
    pallas_call x1, Pallas kernels, per_device(): pl.pallas_call(local_kernel, out_shape=[blocks(capacity), right_blocks],...  3.81 us
    pallas_call x1, Pallas kernels, per_device(): pl.pallas_call(last_kernel, out_shape=[blocks(last), blocks(capacity)], i...  3.07 us
  transfers between devices with their start and end apart: 20, of which 10 were waited for; matrix products, arithmetic and copies ran while one was open for 2% of the time, Pallas kernels for 18%

profile of v2, /device:TPU:24, one launch (start us, length us, event | category | flops | bytes accessed | tf_op | source)
XLA Modules:
  0.0 80.3 jit_solution(98803356261461260)
XLA Ops:
  0.0 6.5 %first_exports.1 = (bf16[8,512,512]{2,1,0:T(8,128)(2,1)S(1)}, bf16[12,512,512]{2,1,0:T(8,128)(2,1)S(1)}, bf16[5,512,512]{2,1,0:T(8,128)(2,1)S(1)}, s32[192]{0:T(256)S(4)}) custom-call(s32[2,12]{1,0:T(2,128)} %routes_in.1, s32[12]{0:T(128)} %live_in.1, bf16[12,512,512]{2,1,0:T(8,128)(2,1)} %psi.1, bf16[2,12,512,512]{3,2,1,0:T(8,128)(2,1)} %left.3), custom_call_target="tpu_custom_call" | custom-call | flops 2147483648 | bytes 13631488 | tf_op jit(solution)/shard_map/first_exports/pallas_call | solution.py:269
  6.6 3.1 %last_exports.1 = (bf16[5,512,512]{2,1,0:T(8,128)(2,1)S(1)}, bf16[13,512,512]{2,1,0:T(8,128)(2,1)S(1)}) custom-call(s32[192]{0:T(256)S(4)} %get-tuple-element.21.plan.refs_0_, bf16[12,512,512]{2,1,0:T(8,128)(2,1)S(1)} %get-tuple-element.22.psi_live, bf16[5,512,512]{2,1,0:T(8,128)(2,1)S(1)} %get-tuple-element.23.ahead, bf16[2,12,512,512]{3,2,1,0:T(8,128)(2,1)} %left.3), custom_call_target="tpu_custom_call" | custom-call | flops 1342177280 | bytes 6815744 | tf_op jit(solution)/shard_map/last_exports/pallas_call | solution.py:291
  9.7 0.5 collective-permute-start.7
  10.2 3.8 %local_mixed.1 = (bf16[13,512,512]{2,1,0:T(8,128)(2,1)S(1)}, bf16[4,1024,512]{2,1,0:T(8,128)(2,1)S(1)}) custom-call(s32[192]{0:T(256)S(4)} %get-tuple-element.21.plan.refs_0_, bf16[12,512,512]{2,1,0:T(8,128)(2,1)S(1)} %get-tuple-element.22.psi_live, bf16[13,512,512]{2,1,0:T(8,128)(2,1)S(1)} %get-tuple-element.24.left_local, bf16[2,12,512,512]{3,2,1,0:T(8,128)(2,1)} %refs_5_.1), custom_call_target="tpu_custom_call" | custom-call | flops 3489660928 | bytes 12582912 | tf_op jit(solution)/shard_map/local_mixed/pallas_call | solution.py:305
  14.0 2.7 %part_sums.3 = (bf16[32,32,512]{2,1,0:T(8,128)(2,1)S(1)}, f32[32,32,512]{2,1,0:T(8,128)S(1)}, bf16[4,1024,512]{2,1,0:T(8,128)(2,1)S(1)}) custom-call(s32[192]{0:T(256)S(4)} %get-tuple-element.21.plan.refs_0_, bf16[13,512,512]{2,1,0:T(8,128)(2,1)S(1)} %get-tuple-element.25.refs_1_, bf16[8,512,512]{2,1,0:T(8,128)(2,1)S(1)} %collective-permute-done.refs_2_, ...), custom_call_target="tpu_custom_call" | custom-call | flops 21474836480 | bytes 4194304 | tf_op jit(solution)/shard_map/part_sums/pallas_call | solution.py:321
  16.7 2.0 %collective-permute-start.1 = (bf16[32,32,512]{2,1,0:T(8,128)(2,1)S(1)}, bf16[32,32,512]{2,1,0:T(8,128)(2,1)S(1)}, u32[]{:S(2)}, u32[]{:S(2)}) collective-permute-start(bf16[32,32,512]{2,1,0:T(8,128)(2,1)S(1)} %get-tuple-element.29), channel_id=1, source_target_pairs={{0,16},{1,17},{2,18},{3,19},{4,20},{5,21},{6,22},{7,23},{8,24},{9,... | collective-permute-start | bytes 3145736 | tf_op jit(solution)/shard_map/ppermute | solution.py:341
  18.7 2.7 %part_sums.4 = (bf16[32,32,512]{2,1,0:T(8,128)(2,1)S(1)}, f32[32,32,512]{2,1,0:T(8,128)S(1)}, bf16[4,1024,512]{2,1,0:T(8,128)(2,1)S(1)}) custom-call(s32[192]{0:T(256)S(4)} %get-tuple-element.21.plan.refs_0_, bf16[13,512,512]{2,1,0:T(8,128)(2,1)S(1)} %get-tuple-element.25.refs_1_, bf16[8,512,512]{2,1,0:T(8,128)(2,1)S(1)} %collective-permute-done.refs_2_, ...), custom_call_target="tpu_custom_call" | custom-call | flops 21474836480 | bytes 4194304 | tf_op jit(solution)/shard_map/part_sums/pallas_call | solution.py:321
  21.4 0.9 %collective-permute-start.8 = (bf16[32,32,512]{2,1,0:T(8,128)(2,1)S(1)}, bf16[32,32,512]{2,1,0:T(8,128)(2,1)S(1)}, u32[]{:S(2)}, u32[]{:S(2)}) collective-permute-start(bf16[32,32,512]{2,1,0:T(8,128)(2,1)S(1)} %get-tuple-element.33), channel_id=1, source_target_pairs={{0,4},{1,5},{2,6},{3,7},{4,0},{5,1},{6,2},{7,3},{8,12},{9,13},{10,... | collective-permute-start | bytes 3145736 | tf_op jit(solution)/shard_map/ppermute | solution.py:341
  22.4 2.6 %part_sums.5 = (bf16[32,32,512]{2,1,0:T(8,128)(2,1)S(1)}, f32[32,32,512]{2,1,0:T(8,128)S(1)}) custom-call(s32[192]{0:T(256)S(4)} %get-tuple-element.21.plan.refs_0_, bf16[13,512,512]{2,1,0:T(8,128)(2,1)S(1)} %get-tuple-element.25.refs_1_, bf16[8,512,512]{2,1,0:T(8,128)(2,1)S(1)} %collective-permute-done.refs_2_, ...), custom_call_target="tpu_custom_call" | custom-call | flops 21474836480 | bytes 4194304 | tf_op jit(solution)/shard_map/part_sums/pallas_call | solution.py:321
  25.0 1.6 %collective-permute-start.14 = (bf16[32,32,512]{2,1,0:T(8,128)(2,1)S(1)}, bf16[32,32,512]{2,1,0:T(8,128)(2,1)S(1)}, u32[]{:S(2)}, u32[]{:S(2)}) collective-permute-start(bf16[32,32,512]{2,1,0:T(8,128)(2,1)S(1)} %get-tuple-element.36), channel_id=1, source_target_pairs={{0,1},{1,0},{2,3},{3,2},{4,5},{5,4},{6,7},{7,6},{8,9},{9,8},{10,11... | collective-permute-start | bytes 3145736 | tf_op jit(solution)/shard_map/ppermute | solution.py:341
  26.5 5.1 %collective-permute-done.1 = bf16[32,32,512]{2,1,0:T(8,128)(2,1)S(1)} collective-permute-done((bf16[32,32,512]{2,1,0:T(8,128)(2,1)S(1)}, bf16[32,32,512]{2,1,0:T(8,128)(2,1)S(1)}, u32[]{:S(2)}, u32[]{:S(2)}) %collective-permute-start.1) | collective-permute-done | bytes 1048608 | tf_op jit(solution)/shard_map/ppermute | solution.py:341
  32.0 4.1 %collective-permute-start.2 = (bf16[16,32,512]{2,1,0:T(8,128)(2,1)S(1)}, bf16[16,32,512]{2,1,0:T(8,128)(2,1)S(1)}, u32[]{:S(2)}, u32[]{:S(2)}) collective-permute-start(bf16[16,32,512]{2,1,0:T(8,128)(2,1)S(1)} %get-tuple-element.37), channel_id=1, source_target_pairs={{0,48},{1,49},{2,50},{3,51},{4,52},{5,53},{6,54},{7,55},{8,56},{9,... | collective-permute-start | bytes 1572872 | tf_op jit(solution)/shard_map/ppermute | solution.py:350
  37.1 2.7 %collective-permute-done.14 = bf16[32,32,512]{2,1,0:T(8,128)(2,1)S(1)} collective-permute-done((bf16[32,32,512]{2,1,0:T(8,128)(2,1)S(1)}, bf16[32,32,512]{2,1,0:T(8,128)(2,1)S(1)}, u32[]{:S(2)}, u32[]{:S(2)}) %collective-permute-start.14) | collective-permute-done | bytes 1048608 | tf_op jit(solution)/shard_map/ppermute | solution.py:341
  40.2 2.9 %collective-permute-start.15 = (bf16[16,32,512]{2,1,0:T(8,128)(2,1)S(1)}, bf16[16,32,512]{2,1,0:T(8,128)(2,1)S(1)}, u32[]{:S(2)}, u32[]{:S(2)}) collective-permute-start(bf16[16,32,512]{2,1,0:T(8,128)(2,1)S(1)} %get-tuple-element.41), channel_id=1, source_target_pairs={{0,3},{1,2},{2,1},{3,0},{4,7},{5,6},{6,5},{7,4},{8,11},{9,10},{10,... | collective-permute-start | bytes 1572872 | tf_op jit(solution)/shard_map/ppermute | solution.py:350
  43.4 1.1 %collective-permute-start.3 = (bf16[8,32,512]{2,1,0:T(8,128)(2,1)S(1)}, bf16[8,32,512]{2,1,0:T(8,128)(2,1)S(1)}, u32[]{:S(2)}, u32[]{:S(2)}) collective-permute-start(bf16[8,32,512]{2,1,0:T(8,128)(2,1)S(1)} %get-tuple-element.43), channel_id=1, source_target_pairs={{0,4},{1,5},{2,6},{3,7},{4,0},{5,1},{6,2},{7,3},{8,12},{9,13},{10,... | collective-permute-start | bytes 786440 | tf_op jit(solution)/shard_map/ppermute | solution.py:350
  44.6 4.1 %collective-permute-done.9 = bf16[16,32,512]{2,1,0:T(8,128)(2,1)S(1)} collective-permute-done((bf16[16,32,512]{2,1,0:T(8,128)(2,1)S(1)}, bf16[16,32,512]{2,1,0:T(8,128)(2,1)S(1)}, u32[]{:S(2)}, u32[]{:S(2)}) %collective-permute-start.9) | collective-permute-done | bytes 524320 | tf_op jit(solution)/shard_map/ppermute | solution.py:350
  48.9 1.0 %collective-permute-start.10 = (bf16[8,32,512]{2,1,0:T(8,128)(2,1)S(1)}, bf16[8,32,512]{2,1,0:T(8,128)(2,1)S(1)}, u32[]{:S(2)}, u32[]{:S(2)}) collective-permute-start(bf16[8,32,512]{2,1,0:T(8,128)(2,1)S(1)} %get-tuple-element.45), channel_id=1, source_target_pairs={{0,1},{1,0},{2,3},{3,2},{4,5},{5,4},{6,7},{7,6},{8,9},{9,8},{10,11... | collective-permute-start | bytes 786440 | tf_op jit(solution)/shard_map/ppermute | solution.py:350
  49.9 0.8 collective-permute-done.15
  50.8 0.8 collective-permute-start.16
  51.7 1.6 %collective-permute-start.4 = (bf16[4,32,512]{2,1,0:T(8,128)(2,1)S(1)}, bf16[4,32,512]{2,1,0:T(8,128)(2,1)S(1)}, u32[]{:S(2)}, u32[]{:S(2)}) collective-permute-start(bf16[4,32,512]{2,1,0:T(8,128)(2,1)S(1)} %get-tuple-element.49), channel_id=1, source_target_pairs={{0,12},{1,13},{2,14},{3,15},{4,8},{5,9},{6,10},{7,11},{8,4},{9,5},... | collective-permute-start | bytes 393224 | tf_op jit(solution)/shard_map/ppermute | solution.py:350
  53.3 2.1 %collective-permute-done.10 = bf16[8,32,512]{2,1,0:T(8,128)(2,1)S(1)} collective-permute-done((bf16[8,32,512]{2,1,0:T(8,128)(2,1)S(1)}, bf16[8,32,512]{2,1,0:T(8,128)(2,1)S(1)}, u32[]{:S(2)}, u32[]{:S(2)}) %collective-permute-start.10) | collective-permute-done | bytes 262176 | tf_op jit(solution)/shard_map/ppermute | solution.py:350
  55.4 2.6 %collective-permute-start.11 = (bf16[4,32,512]{2,1,0:T(8,128)(2,1)S(1)}, bf16[4,32,512]{2,1,0:T(8,128)(2,1)S(1)}, u32[]{:S(2)}, u32[]{:S(2)}) collective-permute-start(bf16[4,32,512]{2,1,0:T(8,128)(2,1)S(1)} %get-tuple-element.51), channel_id=1, source_target_pairs={{0,3},{1,2},{2,1},{3,0},{4,7},{5,6},{6,5},{7,4},{8,11},{9,10},{10,... | collective-permute-start | bytes 393224 | tf_op jit(solution)/shard_map/ppermute | solution.py:350
  58.1 4.1 %collective-permute-start.17 = (bf16[4,32,512]{2,1,0:T(8,128)(2,1)S(1)}, bf16[4,32,512]{2,1,0:T(8,128)(2,1)S(1)}, u32[]{:S(2)}, u32[]{:S(2)}) collective-permute-start(bf16[4,32,512]{2,1,0:T(8,128)(2,1)S(1)} %get-tuple-element.53), channel_id=1, source_target_pairs={{0,48},{1,49},{2,50},{3,51},{4,52},{5,53},{6,54},{7,55},{8,56},{9,... | collective-permute-start | bytes 393224 | tf_op jit(solution)/shard_map/ppermute | solution.py:350
  62.2 1.0 %collective-permute-start.5 = (bf16[2,32,512]{2,1,0:T(8,128)(2,1)S(1)}, bf16[2,32,512]{2,1,0:T(8,128)(2,1)S(1)}, u32[]{:S(2)}, u32[]{:S(2)}) collective-permute-start(bf16[2,32,512]{2,1,0:T(8,128)(2,1)S(1)} %get-tuple-element.55), channel_id=1, source_target_pairs={{0,1},{1,0},{2,3},{3,2},{4,5},{5,4},{6,7},{7,6},{8,9},{9,8},{10,11... | collective-permute-start | bytes 196616 | tf_op jit(solution)/shard_map/ppermute | solution.py:350
  63.3 1.9 %collective-permute-start.12 = (bf16[2,32,512]{2,1,0:T(8,128)(2,1)S(1)}, bf16[2,32,512]{2,1,0:T(8,128)(2,1)S(1)}, u32[]{:S(2)}, u32[]{:S(2)}) collective-permute-start(bf16[2,32,512]{2,1,0:T(8,128)(2,1)S(1)} %get-tuple-element.57), channel_id=1, source_target_pairs={{0,16},{1,17},{2,18},{3,19},{4,20},{5,21},{6,22},{7,23},{8,24},{9,... | collective-permute-start | bytes 196616 | tf_op jit(solution)/shard_map/ppermute | solution.py:350
  65.2 0.7 collective-permute-done.17
  65.9 2.3 %collective-permute-start.18 = (bf16[2,32,512]{2,1,0:T(8,128)(2,1)S(1)}, bf16[2,32,512]{2,1,0:T(8,128)(2,1)S(1)}, u32[]{:S(2)}, u32[]{:S(2)}) collective-permute-start(bf16[2,32,512]{2,1,0:T(8,128)(2,1)S(1)} %get-tuple-element.59), channel_id=1, source_target_pairs={{0,4},{1,5},{2,6},{3,7},{4,0},{5,1},{6,2},{7,3},{8,12},{9,13},{10,... | collective-permute-start | bytes 196616 | tf_op jit(solution)/shard_map/ppermute | solution.py:350
  68.2 2.9 %collective-permute-start.6 = (bf16[1,32,512]{2,1,0:T(8,128)(2,1)S(1)}, bf16[1,32,512]{2,1,0:T(8,128)(2,1)S(1)}, u32[]{:S(2)}, u32[]{:S(2)}) collective-permute-start(bf16[1,32,512]{2,1,0:T(8,128)(2,1)S(1)} %fusion.15), channel_id=1, source_target_pairs={{0,3},{1,2},{2,1},{3,0},{4,7},{5,6},{6,5},{7,4},{8,11},{9,10},{10,... | collective-permute-start | bytes 98312 | tf_op jit(solution)/shard_map/ppermute | solution.py:350
  71.1 3.3 %collective-permute-start.13 = (bf16[1,32,512]{2,1,0:T(8,128)(2,1)S(1)}, bf16[1,32,512]{2,1,0:T(8,128)(2,1)S(1)}, u32[]{:S(2)}, u32[]{:S(2)}) collective-permute-start(bf16[1,32,512]{2,1,0:T(8,128)(2,1)S(1)} %fusion.12), channel_id=1, source_target_pairs={{0,48},{1,49},{2,50},{3,51},{4,52},{5,53},{6,54},{7,55},{8,56},{9,... | collective-permute-start | bytes 98312 | tf_op jit(solution)/shard_map/ppermute | solution.py:350
  74.5 1.8 %collective-permute-done.13 = bf16[1,32,512]{2,1,0:T(8,128)(2,1)S(1)} collective-permute-done((bf16[1,32,512]{2,1,0:T(8,128)(2,1)S(1)}, bf16[1,32,512]{2,1,0:T(8,128)(2,1)S(1)}, u32[]{:S(2)}, u32[]{:S(2)}) %collective-permute-start.13) | collective-permute-done | bytes 32800 | tf_op jit(solution)/shard_map/ppermute | solution.py:350
  76.3 3.3 %collective-permute-done.19 = bf16[1,32,512]{2,1,0:T(8,128)(2,1)S(1)} collective-permute-done((bf16[1,32,512]{2,1,0:T(8,128)(2,1)S(1)}, bf16[1,32,512]{2,1,0:T(8,128)(2,1)S(1)}, u32[]{:S(2)}, u32[]{:S(2)}) %collective-permute-start.19) | collective-permute-done | bytes 32800 | tf_op jit(solution)/shard_map/ppermute | solution.py:350
  79.6 0.7 pad_maximum_fusion
  (33 shorter events, 3.0 us)
Async XLA Ops:
  6.5 7.5 %collective-permute-start = (bf16[8,512,512]{2,1,0:T(8,128)(2,1)S(1)}, bf16[8,512,512]{2,1,0:T(8,128)(2,1)S(1)}, u32[]{:S(2)}, u32[]{:S(2)}) collective-permute-start(bf16[8,512,512]{2,1,0:T(8,128)(2,1)S(1)} %get-tuple-element.26), channel_id=1, source_target_pairs={{0,64},{64,0},{1,65},{65,1},{2,66},{66,2},{3,67},{67,3},{4,68},{68... | collective-permute-start | bytes 12582920 | tf_op jit(solution)/shard_map/ppermute | solution.py:289
  9.7 9.1 %collective-permute-start.7 = (bf16[5,512,512]{2,1,0:T(8,128)(2,1)S(1)}, bf16[5,512,512]{2,1,0:T(8,128)(2,1)S(1)}, u32[]{:S(2)}, u32[]{:S(2)}) collective-permute-start(bf16[5,512,512]{2,1,0:T(8,128)(2,1)S(1)} %get-tuple-element.30), channel_id=1, source_target_pairs={{0,64},{64,0},{1,65},{65,1},{2,66},{66,2},{3,67},{67,3},{4,68},{68... | collective-permute-start | bytes 7864328 | tf_op jit(solution)/shard_map/ppermute | solution.py:301
  16.7 14.9 %collective-permute-start.1 = (bf16[32,32,512]{2,1,0:T(8,128)(2,1)S(1)}, bf16[32,32,512]{2,1,0:T(8,128)(2,1)S(1)}, u32[]{:S(2)}, u32[]{:S(2)}) collective-permute-start(bf16[32,32,512]{2,1,0:T(8,128)(2,1)S(1)} %get-tuple-element.29), channel_id=1, source_target_pairs={{0,16},{1,17},{2,18},{3,19},{4,20},{5,21},{6,22},{7,23},{8,24},{9,... | collective-permute-start | bytes 3145736 | tf_op jit(solution)/shard_map/ppermute | solution.py:341
  21.4 15.1 %collective-permute-start.8 = (bf16[32,32,512]{2,1,0:T(8,128)(2,1)S(1)}, bf16[32,32,512]{2,1,0:T(8,128)(2,1)S(1)}, u32[]{:S(2)}, u32[]{:S(2)}) collective-permute-start(bf16[32,32,512]{2,1,0:T(8,128)(2,1)S(1)} %get-tuple-element.33), channel_id=1, source_target_pairs={{0,4},{1,5},{2,6},{3,7},{4,0},{5,1},{6,2},{7,3},{8,12},{9,13},{10,... | collective-permute-start | bytes 3145736 | tf_op jit(solution)/shard_map/ppermute | solution.py:341
  25.0 14.9 %collective-permute-start.14 = (bf16[32,32,512]{2,1,0:T(8,128)(2,1)S(1)}, bf16[32,32,512]{2,1,0:T(8,128)(2,1)S(1)}, u32[]{:S(2)}, u32[]{:S(2)}) collective-permute-start(bf16[32,32,512]{2,1,0:T(8,128)(2,1)S(1)} %get-tuple-element.36), channel_id=1, source_target_pairs={{0,1},{1,0},{2,3},{3,2},{4,5},{5,4},{6,7},{7,6},{8,9},{9,8},{10,11... | collective-permute-start | bytes 3145736 | tf_op jit(solution)/shard_map/ppermute | solution.py:341
  32.0 11.3 %collective-permute-start.2 = (bf16[16,32,512]{2,1,0:T(8,128)(2,1)S(1)}, bf16[16,32,512]{2,1,0:T(8,128)(2,1)S(1)}, u32[]{:S(2)}, u32[]{:S(2)}) collective-permute-start(bf16[16,32,512]{2,1,0:T(8,128)(2,1)S(1)} %get-tuple-element.37), channel_id=1, source_target_pairs={{0,48},{1,49},{2,50},{3,51},{4,52},{5,53},{6,54},{7,55},{8,56},{9,... | collective-permute-start | bytes 1572872 | tf_op jit(solution)/shard_map/ppermute | solution.py:350
  36.9 11.8 %collective-permute-start.9 = (bf16[16,32,512]{2,1,0:T(8,128)(2,1)S(1)}, bf16[16,32,512]{2,1,0:T(8,128)(2,1)S(1)}, u32[]{:S(2)}, u32[]{:S(2)}) collective-permute-start(bf16[16,32,512]{2,1,0:T(8,128)(2,1)S(1)} %get-tuple-element.39), channel_id=1, source_target_pairs={{0,12},{1,13},{2,14},{3,15},{4,8},{5,9},{6,10},{7,11},{8,4},{9,5},... | collective-permute-start | bytes 1572872 | tf_op jit(solution)/shard_map/ppermute | solution.py:350
  40.2 10.5 %collective-permute-start.15 = (bf16[16,32,512]{2,1,0:T(8,128)(2,1)S(1)}, bf16[16,32,512]{2,1,0:T(8,128)(2,1)S(1)}, u32[]{:S(2)}, u32[]{:S(2)}) collective-permute-start(bf16[16,32,512]{2,1,0:T(8,128)(2,1)S(1)} %get-tuple-element.41), channel_id=1, source_target_pairs={{0,3},{1,2},{2,1},{3,0},{4,7},{5,6},{6,5},{7,4},{8,11},{9,10},{10,... | collective-permute-start | bytes 1572872 | tf_op jit(solution)/shard_map/ppermute | solution.py:350
  43.4 8.2 %collective-permute-start.3 = (bf16[8,32,512]{2,1,0:T(8,128)(2,1)S(1)}, bf16[8,32,512]{2,1,0:T(8,128)(2,1)S(1)}, u32[]{:S(2)}, u32[]{:S(2)}) collective-permute-start(bf16[8,32,512]{2,1,0:T(8,128)(2,1)S(1)} %get-tuple-element.43), channel_id=1, source_target_pairs={{0,4},{1,5},{2,6},{3,7},{4,0},{5,1},{6,2},{7,3},{8,12},{9,13},{10,... | collective-permute-start | bytes 786440 | tf_op jit(solution)/shard_map/ppermute | solution.py:350
  48.9 6.5 %collective-permute-start.10 = (bf16[8,32,512]{2,1,0:T(8,128)(2,1)S(1)}, bf16[8,32,512]{2,1,0:T(8,128)(2,1)S(1)}, u32[]{:S(2)}, u32[]{:S(2)}) collective-permute-start(bf16[8,32,512]{2,1,0:T(8,128)(2,1)S(1)} %get-tuple-element.45), channel_id=1, source_target_pairs={{0,1},{1,0},{2,3},{3,2},{4,5},{5,4},{6,7},{7,6},{8,9},{9,8},{10,11... | collective-permute-start | bytes 786440 | tf_op jit(solution)/shard_map/ppermute | solution.py:350
  50.8 7.2 %collective-permute-start.16 = (bf16[8,32,512]{2,1,0:T(8,128)(2,1)S(1)}, bf16[8,32,512]{2,1,0:T(8,128)(2,1)S(1)}, u32[]{:S(2)}, u32[]{:S(2)}) collective-permute-start(bf16[8,32,512]{2,1,0:T(8,128)(2,1)S(1)} %get-tuple-element.47), channel_id=1, source_target_pairs={{0,16},{1,17},{2,18},{3,19},{4,20},{5,21},{6,22},{7,23},{8,24},{9,... | collective-permute-start | bytes 786440 | tf_op jit(solution)/shard_map/ppermute | solution.py:350
  51.7 10.5 %collective-permute-start.4 = (bf16[4,32,512]{2,1,0:T(8,128)(2,1)S(1)}, bf16[4,32,512]{2,1,0:T(8,128)(2,1)S(1)}, u32[]{:S(2)}, u32[]{:S(2)}) collective-permute-start(bf16[4,32,512]{2,1,0:T(8,128)(2,1)S(1)} %get-tuple-element.49), channel_id=1, source_target_pairs={{0,12},{1,13},{2,14},{3,15},{4,8},{5,9},{6,10},{7,11},{8,4},{9,5},... | collective-permute-start | bytes 393224 | tf_op jit(solution)/shard_map/ppermute | solution.py:350
  55.4 7.9 %collective-permute-start.11 = (bf16[4,32,512]{2,1,0:T(8,128)(2,1)S(1)}, bf16[4,32,512]{2,1,0:T(8,128)(2,1)S(1)}, u32[]{:S(2)}, u32[]{:S(2)}) collective-permute-start(bf16[4,32,512]{2,1,0:T(8,128)(2,1)S(1)} %get-tuple-element.51), channel_id=1, source_target_pairs={{0,3},{1,2},{2,1},{3,0},{4,7},{5,6},{6,5},{7,4},{8,11},{9,10},{10,... | collective-permute-start | bytes 393224 | tf_op jit(solution)/shard_map/ppermute | solution.py:350
  58.1 7.8 %collective-permute-start.17 = (bf16[4,32,512]{2,1,0:T(8,128)(2,1)S(1)}, bf16[4,32,512]{2,1,0:T(8,128)(2,1)S(1)}, u32[]{:S(2)}, u32[]{:S(2)}) collective-permute-start(bf16[4,32,512]{2,1,0:T(8,128)(2,1)S(1)} %get-tuple-element.53), channel_id=1, source_target_pairs={{0,48},{1,49},{2,50},{3,51},{4,52},{5,53},{6,54},{7,55},{8,56},{9,... | collective-permute-start | bytes 393224 | tf_op jit(solution)/shard_map/ppermute | solution.py:350
  62.2 5.9 %collective-permute-start.5 = (bf16[2,32,512]{2,1,0:T(8,128)(2,1)S(1)}, bf16[2,32,512]{2,1,0:T(8,128)(2,1)S(1)}, u32[]{:S(2)}, u32[]{:S(2)}) collective-permute-start(bf16[2,32,512]{2,1,0:T(8,128)(2,1)S(1)} %get-tuple-element.55), channel_id=1, source_target_pairs={{0,1},{1,0},{2,3},{3,2},{4,5},{5,4},{6,7},{7,6},{8,9},{9,8},{10,11... | collective-permute-start | bytes 196616 | tf_op jit(solution)/shard_map/ppermute | solution.py:350
  63.3 7.7 %collective-permute-start.12 = (bf16[2,32,512]{2,1,0:T(8,128)(2,1)S(1)}, bf16[2,32,512]{2,1,0:T(8,128)(2,1)S(1)}, u32[]{:S(2)}, u32[]{:S(2)}) collective-permute-start(bf16[2,32,512]{2,1,0:T(8,128)(2,1)S(1)} %get-tuple-element.57), channel_id=1, source_target_pairs={{0,16},{1,17},{2,18},{3,19},{4,20},{5,21},{6,22},{7,23},{8,24},{9,... | collective-permute-start | bytes 196616 | tf_op jit(solution)/shard_map/ppermute | solution.py:350
  65.9 8.5 %collective-permute-start.18 = (bf16[2,32,512]{2,1,0:T(8,128)(2,1)S(1)}, bf16[2,32,512]{2,1,0:T(8,128)(2,1)S(1)}, u32[]{:S(2)}, u32[]{:S(2)}) collective-permute-start(bf16[2,32,512]{2,1,0:T(8,128)(2,1)S(1)} %get-tuple-element.59), channel_id=1, source_target_pairs={{0,4},{1,5},{2,6},{3,7},{4,0},{5,1},{6,2},{7,3},{8,12},{9,13},{10,... | collective-permute-start | bytes 196616 | tf_op jit(solution)/shard_map/ppermute | solution.py:350
  68.2 6.3 %collective-permute-start.6 = (bf16[1,32,512]{2,1,0:T(8,128)(2,1)S(1)}, bf16[1,32,512]{2,1,0:T(8,128)(2,1)S(1)}, u32[]{:S(2)}, u32[]{:S(2)}) collective-permute-start(bf16[1,32,512]{2,1,0:T(8,128)(2,1)S(1)} %fusion.15), channel_id=1, source_target_pairs={{0,3},{1,2},{2,1},{3,0},{4,7},{5,6},{6,5},{7,4},{8,11},{9,10},{10,... | collective-permute-start | bytes 98312 | tf_op jit(solution)/shard_map/ppermute | solution.py:350
  71.1 5.2 %collective-permute-start.13 = (bf16[1,32,512]{2,1,0:T(8,128)(2,1)S(1)}, bf16[1,32,512]{2,1,0:T(8,128)(2,1)S(1)}, u32[]{:S(2)}, u32[]{:S(2)}) collective-permute-start(bf16[1,32,512]{2,1,0:T(8,128)(2,1)S(1)} %fusion.12), channel_id=1, source_target_pairs={{0,48},{1,49},{2,50},{3,51},{4,52},{5,53},{6,54},{7,55},{8,56},{9,... | collective-permute-start | bytes 98312 | tf_op jit(solution)/shard_map/ppermute | solution.py:350
  74.4 5.2 %collective-permute-start.19 = (bf16[1,32,512]{2,1,0:T(8,128)(2,1)S(1)}, bf16[1,32,512]{2,1,0:T(8,128)(2,1)S(1)}, u32[]{:S(2)}, u32[]{:S(2)}) collective-permute-start(bf16[1,32,512]{2,1,0:T(8,128)(2,1)S(1)} %fusion.9), channel_id=1, source_target_pairs={{0,12},{1,13},{2,14},{3,15},{4,8},{5,9},{6,10},{7,11},{8,4},{9,5},... | collective-permute-start | bytes 98312 | tf_op jit(solution)/shard_map/ppermute | solution.py:350

commit v3 on v2

--- a/solution.py
+++ b/solution.py
@@ -50,31 +50,25 @@
     for copy in tables:
         copy.start()
 
-    quarter = psi.shape[1] // 4
-
-    def load_psi(j, q):
-        piece = pl.ds(quarter * q, quarter)
-        return pltpu.make_async_copy(psi.at[j, piece, :], psi_live.at[j, piece, :], psi_sem.at[j, q])
-
-    def each_live_quarter(j, do):
-        for q in range(4):
-            pl.when(live[j] > quarter * q)(functools.partial(do, j, q))
+    def load_psi(j):
+        return pltpu.make_async_copy(psi.at[j], psi_live.at[j], psi_sem.at[j])
 
     def want_psi(j):
         @pl.when(state[j] == 0)
         def _():
-            each_live_quarter(j, lambda j, q: load_psi(j, q).start())
+            load_psi(j).start()
             state[j] = 1
 
     def have_psi(j):
         @pl.when(state[j] == 1)
         def _():
-            each_live_quarter(j, lambda j, q: load_psi(j, q).wait())
+            load_psi(j).wait()
             cleared(psi_live, j, live[j])
             state[j] = 2
 
     for j in range(slots):
         state[j] = 0
+
     for t in range(terms):
         for s in range(2 * slots):
             inverse[t, s] = -1
@@ -139,19 +133,6 @@
     waited(left, ahead, ahead_sem)
 
 
-def last_kernel(plan, psi_live, ahead, left, out, left_local, sem):
-    count = out.shape[0]
-
-    @pl.loop(0, left_local.shape[0])
-    def _(i):
-        at = LOCAL + i
-        pltpu.make_async_copy(left.at[plan[at], plan[at + LIST]], left_local.at[i], sem.at[i]).start()
-
-    for i in range(count):
-        out[i] = dot(ahead[i], psi_live[plan[EXPORT + LIST + 13 - count + i]]).astype(BF16)
-    waited(left, left_local, sem)
-
-
 def load_right(right, part, target, sem):
     terms, _, rows, _ = right.shape
     per_part = target.shape[0]
@@ -174,11 +155,30 @@
     return wait
 
 
-def local_kernel(plan, psi_live, left_local, right, out, right_part, sem):
-    wait = load_right(right, 0, right_part, sem)
+def rest_kernel(plan, psi_live, ahead, left, right, out, local, right_part, left_buf, left_sem, right_sem):
+    count = local.shape[0]
+
+    def load_left(i):
+        source = left.at[plan[LOCAL + i], plan[LOCAL + LIST + i]]
+        return pltpu.make_async_copy(source, left_buf.at[i], left_sem.at[i])
+
+    @pl.loop(0, count)
+    def _(i):
+        load_left(i).start()
+
+    wait_right = load_right(right, 0, right_part, right_sem)
+    skip = EXPORT + LIST + count - out.shape[0]
     for i in range(out.shape[0]):
-        out[i] = dot(left_local[i], psi_live[plan[LOCAL + LIST + i]]).astype(BF16)
-    wait()
+        out[i] = dot(ahead[i], psi_live[plan[skip + i]]).astype(BF16)
+    for group in (range(0, 6), range(6, count)):
+
+        @pl.loop(group.start, group.stop)
+        def _(i):
+            load_left(i).wait()
+
+        for i in group:
+            local[i] = dot(left_buf[i], psi_live[plan[LOCAL + LIST + i]]).astype(BF16)
+    wait_right()
 
 
 def ring_places(c, core):
@@ -208,19 +208,26 @@
             came = jnp.where(slot > last, received[1][jnp.clip(slot - last - 1, 0, received[1].shape[0] - 1)], came)
         return jnp.where(here == 1, local_mixed[slot], came)
 
-    for k in range(per_part):
+    def product(k):
         s = part * per_part + k
         for t in range(terms):
             mixed[k, :, rows * t : rows * (t + 1)] = block(s, t)
         total[k] = dot(mixed[k], right_part[k])
-    for pair in range(per_part // 2):
-        for n in range(2 * half):
+
+    def lay_out(pair, numbers):
+        for n in numbers:
             row = pl.multiple_of(rings[0][n // 16] + rings[1][n // 4 % 4] + rings[2][n % 4], 8)
             piece = jnp.concatenate([total[2 * pair + e, pl.ds(row, 8), :] for e in range(2)], axis=0)
             if n < half:
                 keep[n, pl.ds(16 * pair, 16), :] = piece
             else:
                 send[n - half, pl.ds(16 * pair, 16), :] = piece.astype(BF16)
+
+    for k in range(per_part):
+        product(k)
+        if k > 1:
+            lay_out(0, range(half * (k - 2), half * (k - 1)))
+    lay_out(1, range(2 * half))
     if part < PARTS - 1:
         wait()
 
@@ -278,7 +285,7 @@
             pltpu.SMEM((slots,), I32),
             blocks(first),
             pltpu.SemaphoreType.DMA((2,)),
-            pltpu.SemaphoreType.DMA((slots, 4)),
+            pltpu.SemaphoreType.DMA((slots,)),
             pltpu.SemaphoreType.DMA((first,)),
             pltpu.SemaphoreType.DMA((last,)),
         ],
@@ -288,30 +295,19 @@
     )(routes, live, psi, left)
     received = [lax.ppermute(outgoing, "sec", swap)]
 
-    outgoing, left_local = pl.pallas_call(
-        last_kernel,
-        out_shape=[blocks(last), blocks(capacity)],
-        in_specs=[SMEM_SPEC, VMEM_SPEC, VMEM_SPEC, HBM_SPEC],
-        out_specs=[VMEM_SPEC] * 2,
-        scratch_shapes=[pltpu.SemaphoreType.DMA((capacity,))],
-        compiler_params=params(4),
-        cost_estimate=cost(last, capacity),
-        name="last_exports",
-    )(plan, psi_live, ahead, left)
-    received.append(lax.ppermute(outgoing, "sec", swap))
-
     right_blocks = pltpu.VMEM((per_part, terms * rows, cols), BF16)
     right_sem = pltpu.SemaphoreType.DMA((per_part, terms))
-    local_mixed, right_part = pl.pallas_call(
-        local_kernel,
-        out_shape=[blocks(capacity), right_blocks],
-        in_specs=[SMEM_SPEC, VMEM_SPEC, VMEM_SPEC, HBM_SPEC],
-        out_specs=[VMEM_SPEC] * 2,
-        scratch_shapes=[right_sem],
-        compiler_params=params(4),
-        cost_estimate=cost(capacity, items),
-        name="local_mixed",
-    )(plan, psi_live, left_local, right)
+    outgoing, local_mixed, right_part = pl.pallas_call(
+        rest_kernel,
+        out_shape=[blocks(last), blocks(capacity), right_blocks],
+        in_specs=[SMEM_SPEC, VMEM_SPEC, VMEM_SPEC, HBM_SPEC, HBM_SPEC],
+        out_specs=[VMEM_SPEC] * 3,
+        scratch_shapes=[blocks(capacity), pltpu.SemaphoreType.DMA((capacity,)), right_sem],
+        compiler_params=params(12),
+        cost_estimate=cost(last + capacity, capacity + part_items),
+        name="rest_mixed",
+    )(plan, psi_live, ahead, left, right)
+    received.append(lax.ppermute(outgoing, "sec", swap))
 
     partners = partner_lists()
     kept, coming = [], []
@@ -348,8 +344,11 @@
             kept[part] = keep[:half] + come[:half].astype(F32)
             axis = ORDERS[part][step // 2]
             coming[part] = lax.ppermute(send, ("sec", "op"), partners[axis][step % 2])
-    done = [(keep + come.astype(F32)).astype(BF16) for keep, come in zip(kept, coming)]
-    return jnp.concatenate([d.reshape(per_part, 8, cols) for d in done], axis=0)
+    out = jnp.zeros((slots, 8, cols), BF16)
+    for part in range(PARTS):
+        done = (kept[part] + coming[part].astype(F32)).astype(BF16).reshape(per_part, 8, cols)
+        out = lax.dynamic_update_slice(out, done, (part * per_part, 0, 0))
+    return out
 
 
 def solution(mesh):

time: 80.4 us -> 79.5 us (0.989)
  starting transfers between devices: 35.1 us -> 37.5 us
  waiting for transfers between devices: 21.1 us -> 19.2 us
  Pallas kernels: 21.3 us -> 20.3 us
    ppermute x15, starting transfers between devices: 29.9 us -> 32.3 us  [per_device(): coming[part] = lax.ppermute(send, ('sec', 'op'), partners[axis][step % 2])]
    ppermute x15, waiting for transfers between devices: 12.9 us -> 11 us  [per_device(): coming[part] = lax.ppermute(send, ('sec', 'op'), partners[axis][step % 2])]
    pallas_call x2 -> x1, Pallas kernels: 6.88 us -> 6.29 us  [per_device(): pl.pallas_call(rest_kernel, out_shape=[blocks(last), blocks(capacity), ri...]
  transfers between devices with their start and end apart: 20 -> 20, of which waited for: 10 -> 11; matrix products, arithmetic and copies ran while one was open for 2% -> 3% of each run, Pallas kernels for 18% -> 18%
where the time goes in v3:
time: 79.5 us; the launch traced here: 79.9 us
  starting transfers between devices  37.5 us (47%)
  Pallas kernels  20.3 us (26%)
  waiting for transfers between devices  19.2 us (24%)
  other arithmetic  2.65 us (3%)
    ppermute x15, starting transfers between devices, per_device(): coming[part] = lax.ppermute(send, ('sec', 'op'), partners[axis][step % 2])  32.3 us
    ppermute x15, waiting for transfers between devices, per_device(): coming[part] = lax.ppermute(send, ('sec', 'op'), partners[axis][step % 2])  11 us
    ppermute x3, waiting for transfers between devices, per_device(): lax.ppermute(send, ('sec', 'op'), partners[ORDERS[part][0]][0])  7.99 us
    pallas_call x3, Pallas kernels, per_device(): pl.pallas_call(functools.partial(part_kernel, part, ORDERS[part]), out_sh...  7.81 us
    pallas_call x1, Pallas kernels, per_device(): pl.pallas_call(rest_kernel, out_shape=[blocks(last), blocks(capacity), ri...  6.29 us
    pallas_call x1, Pallas kernels, per_device(): pl.pallas_call(first_kernel, out_shape=[blocks(first), blocks(slots), blo...  6.23 us
    ppermute x3, starting transfers between devices, per_device(): lax.ppermute(send, ('sec', 'op'), partners[ORDERS[part][0]][0])  4.54 us
    convert_element_type x15, other arithmetic, per_device(): send = (keep[half:] + come[half:].astype(F32)).astype(BF16)  1.99 us
  transfers between devices with their start and end apart: 20, of which 11 were waited for; matrix products, arithmetic and copies ran while one was open for 3% of the time, Pallas kernels for 18%

profile of v3, /device:TPU:24, one launch (start us, length us, event | category | flops | bytes accessed | tf_op | source)
XLA Modules:
  0.0 79.9 jit_solution(5702482043493905698)
XLA Ops:
  0.0 6.2 %first_exports.1 = (bf16[8,512,512]{2,1,0:T(8,128)(2,1)S(1)}, bf16[12,512,512]{2,1,0:T(8,128)(2,1)S(1)}, bf16[5,512,512]{2,1,0:T(8,128)(2,1)S(1)}, s32[192]{0:T(256)S(4)}) custom-call(s32[2,12]{1,0:T(2,128)} %routes_in.1, s32[12]{0:T(128)} %live_in.1, bf16[12,512,512]{2,1,0:T(8,128)(2,1)} %psi.1, bf16[2,12,512,512]{3,2,1,0:T(8,128)(2,1)} %left.3), custom_call_target="tpu_custom_call" | custom-call | flops 2147483648 | bytes 13631488 | tf_op jit(solution)/shard_map/first_exports/pallas_call | solution.py:276
  6.3 6.3 %rest_mixed.1 = (bf16[5,512,512]{2,1,0:T(8,128)(2,1)S(1)}, bf16[13,512,512]{2,1,0:T(8,128)(2,1)S(1)}, bf16[4,1024,512]{2,1,0:T(8,128)(2,1)S(1)}) custom-call(s32[192]{0:T(256)S(4)} %get-tuple-element.20.plan.refs_0_, bf16[12,512,512]{2,1,0:T(8,128)(2,1)S(1)} %get-tuple-element.21.psi_live, bf16[5,512,512]{2,1,0:T(8,128)(2,1)S(1)} %get-tuple-element.22.ahead, ...), custom_call_target="tpu_custom_call" | custom-call | flops 4831838208 | bytes 11010048 | tf_op jit(solution)/shard_map/rest_mixed/pallas_call | solution.py:300
  12.6 0.6 collective-permute-start.7
  13.5 2.6 %part_sums.3 = (bf16[32,32,512]{2,1,0:T(8,128)(2,1)S(1)}, f32[32,32,512]{2,1,0:T(8,128)S(1)}, bf16[4,1024,512]{2,1,0:T(8,128)(2,1)S(1)}) custom-call(s32[192]{0:T(256)S(4)} %get-tuple-element.20.plan.refs_0_, bf16[13,512,512]{2,1,0:T(8,128)(2,1)S(1)} %get-tuple-element.23.refs_1_, bf16[8,512,512]{2,1,0:T(8,128)(2,1)S(1)} %collective-permute-done.refs_2_, ...), custom_call_target="tpu_custom_call" | custom-call | flops 21474836480 | bytes 4194304 | tf_op jit(solution)/shard_map/part_sums/pallas_call | solution.py:317
  16.1 1.9 %collective-permute-start.1 = (bf16[32,32,512]{2,1,0:T(8,128)(2,1)S(1)}, bf16[32,32,512]{2,1,0:T(8,128)(2,1)S(1)}, u32[]{:S(2)}, u32[]{:S(2)}) collective-permute-start(bf16[32,32,512]{2,1,0:T(8,128)(2,1)S(1)} %get-tuple-element.27), channel_id=1, source_target_pairs={{0,16},{1,17},{2,18},{3,19},{4,20},{5,21},{6,22},{7,23},{8,24},{9,... | collective-permute-start | bytes 3145736 | tf_op jit(solution)/shard_map/ppermute | solution.py:337
  18.0 2.6 %part_sums.4 = (bf16[32,32,512]{2,1,0:T(8,128)(2,1)S(1)}, f32[32,32,512]{2,1,0:T(8,128)S(1)}, bf16[4,1024,512]{2,1,0:T(8,128)(2,1)S(1)}) custom-call(s32[192]{0:T(256)S(4)} %get-tuple-element.20.plan.refs_0_, bf16[13,512,512]{2,1,0:T(8,128)(2,1)S(1)} %get-tuple-element.23.refs_1_, bf16[8,512,512]{2,1,0:T(8,128)(2,1)S(1)} %collective-permute-done.refs_2_, ...), custom_call_target="tpu_custom_call" | custom-call | flops 21474836480 | bytes 4194304 | tf_op jit(solution)/shard_map/part_sums/pallas_call | solution.py:317
  20.6 1.2 %collective-permute-start.8 = (bf16[32,32,512]{2,1,0:T(8,128)(2,1)S(1)}, bf16[32,32,512]{2,1,0:T(8,128)(2,1)S(1)}, u32[]{:S(2)}, u32[]{:S(2)}) collective-permute-start(bf16[32,32,512]{2,1,0:T(8,128)(2,1)S(1)} %get-tuple-element.31), channel_id=1, source_target_pairs={{0,4},{1,5},{2,6},{3,7},{4,0},{5,1},{6,2},{7,3},{8,12},{9,13},{10,... | collective-permute-start | bytes 3145736 | tf_op jit(solution)/shard_map/ppermute | solution.py:337
  21.8 2.5 %part_sums.5 = (bf16[32,32,512]{2,1,0:T(8,128)(2,1)S(1)}, f32[32,32,512]{2,1,0:T(8,128)S(1)}) custom-call(s32[192]{0:T(256)S(4)} %get-tuple-element.20.plan.refs_0_, bf16[13,512,512]{2,1,0:T(8,128)(2,1)S(1)} %get-tuple-element.23.refs_1_, bf16[8,512,512]{2,1,0:T(8,128)(2,1)S(1)} %collective-permute-done.refs_2_, ...), custom_call_target="tpu_custom_call" | custom-call | flops 21474836480 | bytes 4194304 | tf_op jit(solution)/shard_map/part_sums/pallas_call | solution.py:317
  24.3 1.5 %collective-permute-start.14 = (bf16[32,32,512]{2,1,0:T(8,128)(2,1)S(1)}, bf16[32,32,512]{2,1,0:T(8,128)(2,1)S(1)}, u32[]{:S(2)}, u32[]{:S(2)}) collective-permute-start(bf16[32,32,512]{2,1,0:T(8,128)(2,1)S(1)} %get-tuple-element.34), channel_id=1, source_target_pairs={{0,1},{1,0},{2,3},{3,2},{4,5},{5,4},{6,7},{7,6},{8,9},{9,8},{10,11... | collective-permute-start | bytes 3145736 | tf_op jit(solution)/shard_map/ppermute | solution.py:337
  25.9 5.1 %collective-permute-done.1 = bf16[32,32,512]{2,1,0:T(8,128)(2,1)S(1)} collective-permute-done((bf16[32,32,512]{2,1,0:T(8,128)(2,1)S(1)}, bf16[32,32,512]{2,1,0:T(8,128)(2,1)S(1)}, u32[]{:S(2)}, u32[]{:S(2)}) %collective-permute-start.1) | collective-permute-done | bytes 1048608 | tf_op jit(solution)/shard_map/ppermute | solution.py:337
  31.0 0.4 add_convert_fusion.2
  31.4 4.1 %collective-permute-start.2 = (bf16[16,32,512]{2,1,0:T(8,128)(2,1)S(1)}, bf16[16,32,512]{2,1,0:T(8,128)(2,1)S(1)}, u32[]{:S(2)}, u32[]{:S(2)}) collective-permute-start(bf16[16,32,512]{2,1,0:T(8,128)(2,1)S(1)} %get-tuple-element.39), channel_id=1, source_target_pairs={{0,48},{1,49},{2,50},{3,51},{4,52},{5,53},{6,54},{7,55},{8,56},{9,... | collective-permute-start | bytes 1572872 | tf_op jit(solution)/shard_map/ppermute | solution.py:346
  35.7 0.4 add_convert_fusion.1
  36.1 0.4 collective-permute-start.9
  36.6 2.7 %collective-permute-done.14 = bf16[32,32,512]{2,1,0:T(8,128)(2,1)S(1)} collective-permute-done((bf16[32,32,512]{2,1,0:T(8,128)(2,1)S(1)}, bf16[32,32,512]{2,1,0:T(8,128)(2,1)S(1)}, u32[]{:S(2)}, u32[]{:S(2)}) %collective-permute-start.14) | collective-permute-done | bytes 1048608 | tf_op jit(solution)/shard_map/ppermute | solution.py:337
  39.6 2.7 %collective-permute-start.15 = (bf16[16,32,512]{2,1,0:T(8,128)(2,1)S(1)}, bf16[16,32,512]{2,1,0:T(8,128)(2,1)S(1)}, u32[]{:S(2)}, u32[]{:S(2)}) collective-permute-start(bf16[16,32,512]{2,1,0:T(8,128)(2,1)S(1)} %get-tuple-element.35), channel_id=1, source_target_pairs={{0,3},{1,2},{2,1},{3,0},{4,7},{5,6},{6,5},{7,4},{8,11},{9,10},{10,... | collective-permute-start | bytes 1572872 | tf_op jit(solution)/shard_map/ppermute | solution.py:346
  42.3 0.4 collective-permute-done.2
  42.8 1.1 %collective-permute-start.3 = (bf16[8,32,512]{2,1,0:T(8,128)(2,1)S(1)}, bf16[8,32,512]{2,1,0:T(8,128)(2,1)S(1)}, u32[]{:S(2)}, u32[]{:S(2)}) collective-permute-start(bf16[8,32,512]{2,1,0:T(8,128)(2,1)S(1)} %get-tuple-element.45), channel_id=1, source_target_pairs={{0,4},{1,5},{2,6},{3,7},{4,0},{5,1},{6,2},{7,3},{8,12},{9,13},{10,... | collective-permute-start | bytes 786440 | tf_op jit(solution)/shard_map/ppermute | solution.py:346
  43.9 3.8 %collective-permute-done.9 = bf16[16,32,512]{2,1,0:T(8,128)(2,1)S(1)} collective-permute-done((bf16[16,32,512]{2,1,0:T(8,128)(2,1)S(1)}, bf16[16,32,512]{2,1,0:T(8,128)(2,1)S(1)}, u32[]{:S(2)}, u32[]{:S(2)}) %collective-permute-start.9) | collective-permute-done | bytes 524320 | tf_op jit(solution)/shard_map/ppermute | solution.py:346
  48.0 1.7 %collective-permute-start.10 = (bf16[8,32,512]{2,1,0:T(8,128)(2,1)S(1)}, bf16[8,32,512]{2,1,0:T(8,128)(2,1)S(1)}, u32[]{:S(2)}, u32[]{:S(2)}) collective-permute-start(bf16[8,32,512]{2,1,0:T(8,128)(2,1)S(1)} %get-tuple-element.43), channel_id=1, source_target_pairs={{0,1},{1,0},{2,3},{3,2},{4,5},{5,4},{6,7},{7,6},{8,9},{9,8},{10,11... | collective-permute-start | bytes 786440 | tf_op jit(solution)/shard_map/ppermute | solution.py:346
  50.2 2.5 %collective-permute-start.16 = (bf16[8,32,512]{2,1,0:T(8,128)(2,1)S(1)}, bf16[8,32,512]{2,1,0:T(8,128)(2,1)S(1)}, u32[]{:S(2)}, u32[]{:S(2)}) collective-permute-start(bf16[8,32,512]{2,1,0:T(8,128)(2,1)S(1)} %get-tuple-element.41), channel_id=1, source_target_pairs={{0,16},{1,17},{2,18},{3,19},{4,20},{5,21},{6,22},{7,23},{8,24},{9,... | collective-permute-start | bytes 786440 | tf_op jit(solution)/shard_map/ppermute | solution.py:346
  52.8 1.2 %collective-permute-start.4 = (bf16[4,32,512]{2,1,0:T(8,128)(2,1)S(1)}, bf16[4,32,512]{2,1,0:T(8,128)(2,1)S(1)}, u32[]{:S(2)}, u32[]{:S(2)}) collective-permute-start(bf16[4,32,512]{2,1,0:T(8,128)(2,1)S(1)} %get-tuple-element.51), channel_id=1, source_target_pairs={{0,12},{1,13},{2,14},{3,15},{4,8},{5,9},{6,10},{7,11},{8,4},{9,5},... | collective-permute-start | bytes 393224 | tf_op jit(solution)/shard_map/ppermute | solution.py:346
  54.5 3.2 %collective-permute-start.11 = (bf16[4,32,512]{2,1,0:T(8,128)(2,1)S(1)}, bf16[4,32,512]{2,1,0:T(8,128)(2,1)S(1)}, u32[]{:S(2)}, u32[]{:S(2)}) collective-permute-start(bf16[4,32,512]{2,1,0:T(8,128)(2,1)S(1)} %get-tuple-element.49), channel_id=1, source_target_pairs={{0,3},{1,2},{2,1},{3,0},{4,7},{5,6},{6,5},{7,4},{8,11},{9,10},{10,... | collective-permute-start | bytes 393224 | tf_op jit(solution)/shard_map/ppermute | solution.py:346
  57.8 5.1 %collective-permute-start.17 = (bf16[4,32,512]{2,1,0:T(8,128)(2,1)S(1)}, bf16[4,32,512]{2,1,0:T(8,128)(2,1)S(1)}, u32[]{:S(2)}, u32[]{:S(2)}) collective-permute-start(bf16[4,32,512]{2,1,0:T(8,128)(2,1)S(1)} %get-tuple-element.47), channel_id=1, source_target_pairs={{0,48},{1,49},{2,50},{3,51},{4,52},{5,53},{6,54},{7,55},{8,56},{9,... | collective-permute-start | bytes 393224 | tf_op jit(solution)/shard_map/ppermute | solution.py:346
  63.0 1.8 %collective-permute-start.12 = (bf16[2,32,512]{2,1,0:T(8,128)(2,1)S(1)}, bf16[2,32,512]{2,1,0:T(8,128)(2,1)S(1)}, u32[]{:S(2)}, u32[]{:S(2)}) collective-permute-start(bf16[2,32,512]{2,1,0:T(8,128)(2,1)S(1)} %get-tuple-element.55), channel_id=1, source_target_pairs={{0,16},{1,17},{2,18},{3,19},{4,20},{5,21},{6,22},{7,23},{8,24},{9,... | collective-permute-start | bytes 196616 | tf_op jit(solution)/shard_map/ppermute | solution.py:346
  64.9 0.9 %collective-permute-done.17 = bf16[4,32,512]{2,1,0:T(8,128)(2,1)S(1)} collective-permute-done((bf16[4,32,512]{2,1,0:T(8,128)(2,1)S(1)}, bf16[4,32,512]{2,1,0:T(8,128)(2,1)S(1)}, u32[]{:S(2)}, u32[]{:S(2)}) %collective-permute-start.17) | collective-permute-done | bytes 131104 | tf_op jit(solution)/shard_map/ppermute | solution.py:346
  65.8 2.3 %collective-permute-start.18 = (bf16[2,32,512]{2,1,0:T(8,128)(2,1)S(1)}, bf16[2,32,512]{2,1,0:T(8,128)(2,1)S(1)}, u32[]{:S(2)}, u32[]{:S(2)}) collective-permute-start(bf16[2,32,512]{2,1,0:T(8,128)(2,1)S(1)} %get-tuple-element.53), channel_id=1, source_target_pairs={{0,4},{1,5},{2,6},{3,7},{4,0},{5,1},{6,2},{7,3},{8,12},{9,13},{10,... | collective-permute-start | bytes 196616 | tf_op jit(solution)/shard_map/ppermute | solution.py:346
  68.1 2.7 %collective-permute-start.6 = (bf16[1,32,512]{2,1,0:T(8,128)(2,1)S(1)}, bf16[1,32,512]{2,1,0:T(8,128)(2,1)S(1)}, u32[]{:S(2)}, u32[]{:S(2)}) collective-permute-start(bf16[1,32,512]{2,1,0:T(8,128)(2,1)S(1)} %fusion.15), channel_id=1, source_target_pairs={{0,3},{1,2},{2,1},{3,0},{4,7},{5,6},{6,5},{7,4},{8,11},{9,10},{10,... | collective-permute-start | bytes 98312 | tf_op jit(solution)/shard_map/ppermute | solution.py:346
  70.8 3.3 %collective-permute-start.13 = (bf16[1,32,512]{2,1,0:T(8,128)(2,1)S(1)}, bf16[1,32,512]{2,1,0:T(8,128)(2,1)S(1)}, u32[]{:S(2)}, u32[]{:S(2)}) collective-permute-start(bf16[1,32,512]{2,1,0:T(8,128)(2,1)S(1)} %fusion.12), channel_id=1, source_target_pairs={{0,48},{1,49},{2,50},{3,51},{4,52},{5,53},{6,54},{7,55},{8,56},{9,... | collective-permute-start | bytes 98312 | tf_op jit(solution)/shard_map/ppermute | solution.py:346
  74.3 1.7 %collective-permute-done.13 = bf16[1,32,512]{2,1,0:T(8,128)(2,1)S(1)} collective-permute-done((bf16[1,32,512]{2,1,0:T(8,128)(2,1)S(1)}, bf16[1,32,512]{2,1,0:T(8,128)(2,1)S(1)}, u32[]{:S(2)}, u32[]{:S(2)}) %collective-permute-start.13) | collective-permute-done | bytes 32800 | tf_op jit(solution)/shard_map/ppermute | solution.py:346
  76.0 3.3 %collective-permute-done.19 = bf16[1,32,512]{2,1,0:T(8,128)(2,1)S(1)} collective-permute-done((bf16[1,32,512]{2,1,0:T(8,128)(2,1)S(1)}, bf16[1,32,512]{2,1,0:T(8,128)(2,1)S(1)}, u32[]{:S(2)}, u32[]{:S(2)}) %collective-permute-start.19) | collective-permute-done | bytes 32800 | tf_op jit(solution)/shard_map/ppermute | solution.py:346
  79.3 0.6 fusion.22
  (34 shorter events, 2.7 us)
Async XLA Ops:
  6.2 7.2 %collective-permute-start = (bf16[8,512,512]{2,1,0:T(8,128)(2,1)S(1)}, bf16[8,512,512]{2,1,0:T(8,128)(2,1)S(1)}, u32[]{:S(2)}, u32[]{:S(2)}) collective-permute-start(bf16[8,512,512]{2,1,0:T(8,128)(2,1)S(1)} %get-tuple-element.24), channel_id=1, source_target_pairs={{0,64},{64,0},{1,65},{65,1},{2,66},{66,2},{3,67},{67,3},{4,68},{68... | collective-permute-start | bytes 12582920 | tf_op jit(solution)/shard_map/ppermute | solution.py:296
  12.6 5.3 %collective-permute-start.7 = (bf16[5,512,512]{2,1,0:T(8,128)(2,1)S(1)}, bf16[5,512,512]{2,1,0:T(8,128)(2,1)S(1)}, u32[]{:S(2)}, u32[]{:S(2)}) collective-permute-start(bf16[5,512,512]{2,1,0:T(8,128)(2,1)S(1)} %get-tuple-element.28), channel_id=1, source_target_pairs={{0,64},{64,0},{1,65},{65,1},{2,66},{66,2},{3,67},{67,3},{4,68},{68... | collective-permute-start | bytes 7864328 | tf_op jit(solution)/shard_map/ppermute | solution.py:310
  16.1 14.9 %collective-permute-start.1 = (bf16[32,32,512]{2,1,0:T(8,128)(2,1)S(1)}, bf16[32,32,512]{2,1,0:T(8,128)(2,1)S(1)}, u32[]{:S(2)}, u32[]{:S(2)}) collective-permute-start(bf16[32,32,512]{2,1,0:T(8,128)(2,1)S(1)} %get-tuple-element.27), channel_id=1, source_target_pairs={{0,16},{1,17},{2,18},{3,19},{4,20},{5,21},{6,22},{7,23},{8,24},{9,... | collective-permute-start | bytes 3145736 | tf_op jit(solution)/shard_map/ppermute | solution.py:337
  20.6 15.1 %collective-permute-start.8 = (bf16[32,32,512]{2,1,0:T(8,128)(2,1)S(1)}, bf16[32,32,512]{2,1,0:T(8,128)(2,1)S(1)}, u32[]{:S(2)}, u32[]{:S(2)}) collective-permute-start(bf16[32,32,512]{2,1,0:T(8,128)(2,1)S(1)} %get-tuple-element.31), channel_id=1, source_target_pairs={{0,4},{1,5},{2,6},{3,7},{4,0},{5,1},{6,2},{7,3},{8,12},{9,13},{10,... | collective-permute-start | bytes 3145736 | tf_op jit(solution)/shard_map/ppermute | solution.py:337
  24.3 14.9 %collective-permute-start.14 = (bf16[32,32,512]{2,1,0:T(8,128)(2,1)S(1)}, bf16[32,32,512]{2,1,0:T(8,128)(2,1)S(1)}, u32[]{:S(2)}, u32[]{:S(2)}) collective-permute-start(bf16[32,32,512]{2,1,0:T(8,128)(2,1)S(1)} %get-tuple-element.34), channel_id=1, source_target_pairs={{0,1},{1,0},{2,3},{3,2},{4,5},{5,4},{6,7},{7,6},{8,9},{9,8},{10,11... | collective-permute-start | bytes 3145736 | tf_op jit(solution)/shard_map/ppermute | solution.py:337
  31.4 11.3 %collective-permute-start.2 = (bf16[16,32,512]{2,1,0:T(8,128)(2,1)S(1)}, bf16[16,32,512]{2,1,0:T(8,128)(2,1)S(1)}, u32[]{:S(2)}, u32[]{:S(2)}) collective-permute-start(bf16[16,32,512]{2,1,0:T(8,128)(2,1)S(1)} %get-tuple-element.39), channel_id=1, source_target_pairs={{0,48},{1,49},{2,50},{3,51},{4,52},{5,53},{6,54},{7,55},{8,56},{9,... | collective-permute-start | bytes 1572872 | tf_op jit(solution)/shard_map/ppermute | solution.py:346
  36.1 11.7 %collective-permute-start.9 = (bf16[16,32,512]{2,1,0:T(8,128)(2,1)S(1)}, bf16[16,32,512]{2,1,0:T(8,128)(2,1)S(1)}, u32[]{:S(2)}, u32[]{:S(2)}) collective-permute-start(bf16[16,32,512]{2,1,0:T(8,128)(2,1)S(1)} %get-tuple-element.37), channel_id=1, source_target_pairs={{0,12},{1,13},{2,14},{3,15},{4,8},{5,9},{6,10},{7,11},{8,4},{9,5},... | collective-permute-start | bytes 1572872 | tf_op jit(solution)/shard_map/ppermute | solution.py:346
  39.6 10.5 %collective-permute-start.15 = (bf16[16,32,512]{2,1,0:T(8,128)(2,1)S(1)}, bf16[16,32,512]{2,1,0:T(8,128)(2,1)S(1)}, u32[]{:S(2)}, u32[]{:S(2)}) collective-permute-start(bf16[16,32,512]{2,1,0:T(8,128)(2,1)S(1)} %get-tuple-element.35), channel_id=1, source_target_pairs={{0,3},{1,2},{2,1},{3,0},{4,7},{5,6},{6,5},{7,4},{8,11},{9,10},{10,... | collective-permute-start | bytes 1572872 | tf_op jit(solution)/shard_map/ppermute | solution.py:346
  42.8 9.9 %collective-permute-start.3 = (bf16[8,32,512]{2,1,0:T(8,128)(2,1)S(1)}, bf16[8,32,512]{2,1,0:T(8,128)(2,1)S(1)}, u32[]{:S(2)}, u32[]{:S(2)}) collective-permute-start(bf16[8,32,512]{2,1,0:T(8,128)(2,1)S(1)} %get-tuple-element.45), channel_id=1, source_target_pairs={{0,4},{1,5},{2,6},{3,7},{4,0},{5,1},{6,2},{7,3},{8,12},{9,13},{10,... | collective-permute-start | bytes 786440 | tf_op jit(solution)/shard_map/ppermute | solution.py:346
  48.0 6.5 %collective-permute-start.10 = (bf16[8,32,512]{2,1,0:T(8,128)(2,1)S(1)}, bf16[8,32,512]{2,1,0:T(8,128)(2,1)S(1)}, u32[]{:S(2)}, u32[]{:S(2)}) collective-permute-start(bf16[8,32,512]{2,1,0:T(8,128)(2,1)S(1)} %get-tuple-element.43), channel_id=1, source_target_pairs={{0,1},{1,0},{2,3},{3,2},{4,5},{5,4},{6,7},{7,6},{8,9},{9,8},{10,11... | collective-permute-start | bytes 786440 | tf_op jit(solution)/shard_map/ppermute | solution.py:346
  50.2 7.5 %collective-permute-start.16 = (bf16[8,32,512]{2,1,0:T(8,128)(2,1)S(1)}, bf16[8,32,512]{2,1,0:T(8,128)(2,1)S(1)}, u32[]{:S(2)}, u32[]{:S(2)}) collective-permute-start(bf16[8,32,512]{2,1,0:T(8,128)(2,1)S(1)} %get-tuple-element.41), channel_id=1, source_target_pairs={{0,16},{1,17},{2,18},{3,19},{4,20},{5,21},{6,22},{7,23},{8,24},{9,... | collective-permute-start | bytes 786440 | tf_op jit(solution)/shard_map/ppermute | solution.py:346
  52.8 10.0 %collective-permute-start.4 = (bf16[4,32,512]{2,1,0:T(8,128)(2,1)S(1)}, bf16[4,32,512]{2,1,0:T(8,128)(2,1)S(1)}, u32[]{:S(2)}, u32[]{:S(2)}) collective-permute-start(bf16[4,32,512]{2,1,0:T(8,128)(2,1)S(1)} %get-tuple-element.51), channel_id=1, source_target_pairs={{0,12},{1,13},{2,14},{3,15},{4,8},{5,9},{6,10},{7,11},{8,4},{9,5},... | collective-permute-start | bytes 393224 | tf_op jit(solution)/shard_map/ppermute | solution.py:346
  54.5 8.5 %collective-permute-start.11 = (bf16[4,32,512]{2,1,0:T(8,128)(2,1)S(1)}, bf16[4,32,512]{2,1,0:T(8,128)(2,1)S(1)}, u32[]{:S(2)}, u32[]{:S(2)}) collective-permute-start(bf16[4,32,512]{2,1,0:T(8,128)(2,1)S(1)} %get-tuple-element.49), channel_id=1, source_target_pairs={{0,3},{1,2},{2,1},{3,0},{4,7},{5,6},{6,5},{7,4},{8,11},{9,10},{10,... | collective-permute-start | bytes 393224 | tf_op jit(solution)/shard_map/ppermute | solution.py:346
  57.8 8.0 %collective-permute-start.17 = (bf16[4,32,512]{2,1,0:T(8,128)(2,1)S(1)}, bf16[4,32,512]{2,1,0:T(8,128)(2,1)S(1)}, u32[]{:S(2)}, u32[]{:S(2)}) collective-permute-start(bf16[4,32,512]{2,1,0:T(8,128)(2,1)S(1)} %get-tuple-element.47), channel_id=1, source_target_pairs={{0,48},{1,49},{2,50},{3,51},{4,52},{5,53},{6,54},{7,55},{8,56},{9,... | collective-permute-start | bytes 393224 | tf_op jit(solution)/shard_map/ppermute | solution.py:346
  62.9 5.2 %collective-permute-start.5 = (bf16[2,32,512]{2,1,0:T(8,128)(2,1)S(1)}, bf16[2,32,512]{2,1,0:T(8,128)(2,1)S(1)}, u32[]{:S(2)}, u32[]{:S(2)}) collective-permute-start(bf16[2,32,512]{2,1,0:T(8,128)(2,1)S(1)} %get-tuple-element.57), channel_id=1, source_target_pairs={{0,1},{1,0},{2,3},{3,2},{4,5},{5,4},{6,7},{7,6},{8,9},{9,8},{10,11... | collective-permute-start | bytes 196616 | tf_op jit(solution)/shard_map/ppermute | solution.py:346
  63.0 7.7 %collective-permute-start.12 = (bf16[2,32,512]{2,1,0:T(8,128)(2,1)S(1)}, bf16[2,32,512]{2,1,0:T(8,128)(2,1)S(1)}, u32[]{:S(2)}, u32[]{:S(2)}) collective-permute-start(bf16[2,32,512]{2,1,0:T(8,128)(2,1)S(1)} %get-tuple-element.55), channel_id=1, source_target_pairs={{0,16},{1,17},{2,18},{3,19},{4,20},{5,21},{6,22},{7,23},{8,24},{9,... | collective-permute-start | bytes 196616 | tf_op jit(solution)/shard_map/ppermute | solution.py:346
  65.8 8.3 %collective-permute-start.18 = (bf16[2,32,512]{2,1,0:T(8,128)(2,1)S(1)}, bf16[2,32,512]{2,1,0:T(8,128)(2,1)S(1)}, u32[]{:S(2)}, u32[]{:S(2)}) collective-permute-start(bf16[2,32,512]{2,1,0:T(8,128)(2,1)S(1)} %get-tuple-element.53), channel_id=1, source_target_pairs={{0,4},{1,5},{2,6},{3,7},{4,0},{5,1},{6,2},{7,3},{8,12},{9,13},{10,... | collective-permute-start | bytes 196616 | tf_op jit(solution)/shard_map/ppermute | solution.py:346
  68.1 6.1 %collective-permute-start.6 = (bf16[1,32,512]{2,1,0:T(8,128)(2,1)S(1)}, bf16[1,32,512]{2,1,0:T(8,128)(2,1)S(1)}, u32[]{:S(2)}, u32[]{:S(2)}) collective-permute-start(bf16[1,32,512]{2,1,0:T(8,128)(2,1)S(1)} %fusion.15), channel_id=1, source_target_pairs={{0,3},{1,2},{2,1},{3,0},{4,7},{5,6},{6,5},{7,4},{8,11},{9,10},{10,... | collective-permute-start | bytes 98312 | tf_op jit(solution)/shard_map/ppermute | solution.py:346
  70.8 5.2 %collective-permute-start.13 = (bf16[1,32,512]{2,1,0:T(8,128)(2,1)S(1)}, bf16[1,32,512]{2,1,0:T(8,128)(2,1)S(1)}, u32[]{:S(2)}, u32[]{:S(2)}) collective-permute-start(bf16[1,32,512]{2,1,0:T(8,128)(2,1)S(1)} %fusion.12), channel_id=1, source_target_pairs={{0,48},{1,49},{2,50},{3,51},{4,52},{5,53},{6,54},{7,55},{8,56},{9,... | collective-permute-start | bytes 98312 | tf_op jit(solution)/shard_map/ppermute | solution.py:346
  74.1 5.2 %collective-permute-start.19 = (bf16[1,32,512]{2,1,0:T(8,128)(2,1)S(1)}, bf16[1,32,512]{2,1,0:T(8,128)(2,1)S(1)}, u32[]{:S(2)}, u32[]{:S(2)}) collective-permute-start(bf16[1,32,512]{2,1,0:T(8,128)(2,1)S(1)} %fusion.9), channel_id=1, source_target_pairs={{0,12},{1,13},{2,14},{3,15},{4,8},{5,9},{6,10},{7,11},{8,4},{9,5},... | collective-permute-start | bytes 98312 | tf_op jit(solution)/shard_map/ppermute | solution.py:346
  76.0 3.3 %copy-start = (bf16[12,8,512]{2,1,0:T(8,128)(2,1)}, bf16[12,8,512]{2,1,0:T(8,128)(2,1)S(1)}, u32[]{:S(2)}) copy-start(bf16[12,8,512]{2,1,0:T(8,128)(2,1)S(1)} %fusion.20) | copy-start | bytes 294916

commit v4 on v3

--- a/solution.py
+++ b/solution.py
@@ -122,7 +122,7 @@
             plan[SLOT + terms * s + t] = jnp.where(here == 1, local_count, other_count)
             local_count = local_count + here
             other_count = other_count + 1 - here
-    for group in (range(first // 2), range(first // 2, first)):
+    for group in (range(2), range(2, 5), range(5, first)):
         for i in group:
             have_psi(plan[EXPORT + LIST + i])
             load_left(i).wait()

time: 79.5 us -> 79.2 us (level)
  transfers between devices with their start and end apart: 20 -> 20, of which waited for: 11 -> 10; matrix products, arithmetic and copies ran while one was open for 3% -> 3% of each run, Pallas kernels for 18% -> 18%
where the time goes in v4:
time: 79.2 us; the launch traced here: 79.3 us
  starting transfers between devices  37.6 us (47%)
  Pallas kernels  20.1 us (25%)
  waiting for transfers between devices  18.8 us (24%)
  other arithmetic  2.65 us (3%)
    ppermute x15, starting transfers between devices, per_device(): coming[part] = lax.ppermute(send, ('sec', 'op'), partners[axis][step % 2])  32.4 us
    ppermute x15, waiting for transfers between devices, per_device(): coming[part] = lax.ppermute(send, ('sec', 'op'), partners[axis][step % 2])  10.5 us
    ppermute x3, waiting for transfers between devices, per_device(): lax.ppermute(send, ('sec', 'op'), partners[ORDERS[part][0]][0])  8.04 us
    pallas_call x3, Pallas kernels, per_device(): pl.pallas_call(functools.partial(part_kernel, part, ORDERS[part]), out_sh...  7.81 us
    pallas_call x1, Pallas kernels, per_device(): pl.pallas_call(rest_kernel, out_shape=[blocks(last), blocks(capacity), ri...  6.36 us
    pallas_call x1, Pallas kernels, per_device(): pl.pallas_call(first_kernel, out_shape=[blocks(first), blocks(slots), blo...  5.89 us
    ppermute x3, starting transfers between devices, per_device(): lax.ppermute(send, ('sec', 'op'), partners[ORDERS[part][0]][0])  4.56 us
    convert_element_type x15, other arithmetic, per_device(): send = (keep[half:] + come[half:].astype(F32)).astype(BF16)  1.99 us
  transfers between devices with their start and end apart: 20, of which 10 were waited for; matrix products, arithmetic and copies ran while one was open for 3% of the time, Pallas kernels for 18%

profile of v4, /device:TPU:24, one launch (start us, length us, event | category | flops | bytes accessed | tf_op | source)
XLA Modules:
  0.0 79.3 jit_solution(11501350730772571232)
XLA Ops:
  0.0 5.9 %first_exports.1 = (bf16[8,512,512]{2,1,0:T(8,128)(2,1)S(1)}, bf16[12,512,512]{2,1,0:T(8,128)(2,1)S(1)}, bf16[5,512,512]{2,1,0:T(8,128)(2,1)S(1)}, s32[192]{0:T(256)S(4)}) custom-call(s32[2,12]{1,0:T(2,128)} %routes_in.1, s32[12]{0:T(128)} %live_in.1, bf16[12,512,512]{2,1,0:T(8,128)(2,1)} %psi.1, bf16[2,12,512,512]{3,2,1,0:T(8,128)(2,1)} %left.3), custom_call_target="tpu_custom_call" | custom-call | flops 2147483648 | bytes 13631488 | tf_op jit(solution)/shard_map/first_exports/pallas_call | solution.py:276
  6.0 6.4 %rest_mixed.1 = (bf16[5,512,512]{2,1,0:T(8,128)(2,1)S(1)}, bf16[13,512,512]{2,1,0:T(8,128)(2,1)S(1)}, bf16[4,1024,512]{2,1,0:T(8,128)(2,1)S(1)}) custom-call(s32[192]{0:T(256)S(4)} %get-tuple-element.20.plan.refs_0_, bf16[12,512,512]{2,1,0:T(8,128)(2,1)S(1)} %get-tuple-element.21.psi_live, bf16[5,512,512]{2,1,0:T(8,128)(2,1)S(1)} %get-tuple-element.22.ahead, ...), custom_call_target="tpu_custom_call" | custom-call | flops 4831838208 | bytes 11010048 | tf_op jit(solution)/shard_map/rest_mixed/pallas_call | solution.py:300
  12.4 0.6 collective-permute-start.7
  13.1 2.6 %part_sums.3 = (bf16[32,32,512]{2,1,0:T(8,128)(2,1)S(1)}, f32[32,32,512]{2,1,0:T(8,128)S(1)}, bf16[4,1024,512]{2,1,0:T(8,128)(2,1)S(1)}) custom-call(s32[192]{0:T(256)S(4)} %get-tuple-element.20.plan.refs_0_, bf16[13,512,512]{2,1,0:T(8,128)(2,1)S(1)} %get-tuple-element.23.refs_1_, bf16[8,512,512]{2,1,0:T(8,128)(2,1)S(1)} %collective-permute-done.refs_2_, ...), custom_call_target="tpu_custom_call" | custom-call | flops 21474836480 | bytes 4194304 | tf_op jit(solution)/shard_map/part_sums/pallas_call | solution.py:317
  15.8 2.0 %collective-permute-start.1 = (bf16[32,32,512]{2,1,0:T(8,128)(2,1)S(1)}, bf16[32,32,512]{2,1,0:T(8,128)(2,1)S(1)}, u32[]{:S(2)}, u32[]{:S(2)}) collective-permute-start(bf16[32,32,512]{2,1,0:T(8,128)(2,1)S(1)} %get-tuple-element.27), channel_id=1, source_target_pairs={{0,16},{1,17},{2,18},{3,19},{4,20},{5,21},{6,22},{7,23},{8,24},{9,... | collective-permute-start | bytes 3145736 | tf_op jit(solution)/shard_map/ppermute | solution.py:337
  17.8 2.6 %part_sums.4 = (bf16[32,32,512]{2,1,0:T(8,128)(2,1)S(1)}, f32[32,32,512]{2,1,0:T(8,128)S(1)}, bf16[4,1024,512]{2,1,0:T(8,128)(2,1)S(1)}) custom-call(s32[192]{0:T(256)S(4)} %get-tuple-element.20.plan.refs_0_, bf16[13,512,512]{2,1,0:T(8,128)(2,1)S(1)} %get-tuple-element.23.refs_1_, bf16[8,512,512]{2,1,0:T(8,128)(2,1)S(1)} %collective-permute-done.refs_2_, ...), custom_call_target="tpu_custom_call" | custom-call | flops 21474836480 | bytes 4194304 | tf_op jit(solution)/shard_map/part_sums/pallas_call | solution.py:317
  20.4 1.0 %collective-permute-start.8 = (bf16[32,32,512]{2,1,0:T(8,128)(2,1)S(1)}, bf16[32,32,512]{2,1,0:T(8,128)(2,1)S(1)}, u32[]{:S(2)}, u32[]{:S(2)}) collective-permute-start(bf16[32,32,512]{2,1,0:T(8,128)(2,1)S(1)} %get-tuple-element.31), channel_id=1, source_target_pairs={{0,4},{1,5},{2,6},{3,7},{4,0},{5,1},{6,2},{7,3},{8,12},{9,13},{10,... | collective-permute-start | bytes 3145736 | tf_op jit(solution)/shard_map/ppermute | solution.py:337
  21.4 2.5 %part_sums.5 = (bf16[32,32,512]{2,1,0:T(8,128)(2,1)S(1)}, f32[32,32,512]{2,1,0:T(8,128)S(1)}) custom-call(s32[192]{0:T(256)S(4)} %get-tuple-element.20.plan.refs_0_, bf16[13,512,512]{2,1,0:T(8,128)(2,1)S(1)} %get-tuple-element.23.refs_1_, bf16[8,512,512]{2,1,0:T(8,128)(2,1)S(1)} %collective-permute-done.refs_2_, ...), custom_call_target="tpu_custom_call" | custom-call | flops 21474836480 | bytes 4194304 | tf_op jit(solution)/shard_map/part_sums/pallas_call | solution.py:317
  23.9 1.6 %collective-permute-start.14 = (bf16[32,32,512]{2,1,0:T(8,128)(2,1)S(1)}, bf16[32,32,512]{2,1,0:T(8,128)(2,1)S(1)}, u32[]{:S(2)}, u32[]{:S(2)}) collective-permute-start(bf16[32,32,512]{2,1,0:T(8,128)(2,1)S(1)} %get-tuple-element.34), channel_id=1, source_target_pairs={{0,1},{1,0},{2,3},{3,2},{4,5},{5,4},{6,7},{7,6},{8,9},{9,8},{10,11... | collective-permute-start | bytes 3145736 | tf_op jit(solution)/shard_map/ppermute | solution.py:337
  25.5 5.1 %collective-permute-done.1 = bf16[32,32,512]{2,1,0:T(8,128)(2,1)S(1)} collective-permute-done((bf16[32,32,512]{2,1,0:T(8,128)(2,1)S(1)}, bf16[32,32,512]{2,1,0:T(8,128)(2,1)S(1)}, u32[]{:S(2)}, u32[]{:S(2)}) %collective-permute-start.1) | collective-permute-done | bytes 1048608 | tf_op jit(solution)/shard_map/ppermute | solution.py:337
  30.7 0.4 add_convert_fusion.2
  31.0 4.1 %collective-permute-start.2 = (bf16[16,32,512]{2,1,0:T(8,128)(2,1)S(1)}, bf16[16,32,512]{2,1,0:T(8,128)(2,1)S(1)}, u32[]{:S(2)}, u32[]{:S(2)}) collective-permute-start(bf16[16,32,512]{2,1,0:T(8,128)(2,1)S(1)} %get-tuple-element.39), channel_id=1, source_target_pairs={{0,48},{1,49},{2,50},{3,51},{4,52},{5,53},{6,54},{7,55},{8,56},{9,... | collective-permute-start | bytes 1572872 | tf_op jit(solution)/shard_map/ppermute | solution.py:346
  35.5 0.4 add_convert_fusion.1
  36.2 2.6 %collective-permute-done.14 = bf16[32,32,512]{2,1,0:T(8,128)(2,1)S(1)} collective-permute-done((bf16[32,32,512]{2,1,0:T(8,128)(2,1)S(1)}, bf16[32,32,512]{2,1,0:T(8,128)(2,1)S(1)}, u32[]{:S(2)}, u32[]{:S(2)}) %collective-permute-start.14) | collective-permute-done | bytes 1048608 | tf_op jit(solution)/shard_map/ppermute | solution.py:337
  38.8 0.3 add_convert_fusion
  39.2 2.9 %collective-permute-start.15 = (bf16[16,32,512]{2,1,0:T(8,128)(2,1)S(1)}, bf16[16,32,512]{2,1,0:T(8,128)(2,1)S(1)}, u32[]{:S(2)}, u32[]{:S(2)}) collective-permute-start(bf16[16,32,512]{2,1,0:T(8,128)(2,1)S(1)} %get-tuple-element.35), channel_id=1, source_target_pairs={{0,3},{1,2},{2,1},{3,0},{4,7},{5,6},{6,5},{7,4},{8,11},{9,10},{10,... | collective-permute-start | bytes 1572872 | tf_op jit(solution)/shard_map/ppermute | solution.py:346
  42.5 1.1 %collective-permute-start.3 = (bf16[8,32,512]{2,1,0:T(8,128)(2,1)S(1)}, bf16[8,32,512]{2,1,0:T(8,128)(2,1)S(1)}, u32[]{:S(2)}, u32[]{:S(2)}) collective-permute-start(bf16[8,32,512]{2,1,0:T(8,128)(2,1)S(1)} %get-tuple-element.45), channel_id=1, source_target_pairs={{0,4},{1,5},{2,6},{3,7},{4,0},{5,1},{6,2},{7,3},{8,12},{9,13},{10,... | collective-permute-start | bytes 786440 | tf_op jit(solution)/shard_map/ppermute | solution.py:346
  43.6 4.1 %collective-permute-done.9 = bf16[16,32,512]{2,1,0:T(8,128)(2,1)S(1)} collective-permute-done((bf16[16,32,512]{2,1,0:T(8,128)(2,1)S(1)}, bf16[16,32,512]{2,1,0:T(8,128)(2,1)S(1)}, u32[]{:S(2)}, u32[]{:S(2)}) %collective-permute-start.9) | collective-permute-done | bytes 524320 | tf_op jit(solution)/shard_map/ppermute | solution.py:346
  47.8 1.5 %collective-permute-start.10 = (bf16[8,32,512]{2,1,0:T(8,128)(2,1)S(1)}, bf16[8,32,512]{2,1,0:T(8,128)(2,1)S(1)}, u32[]{:S(2)}, u32[]{:S(2)}) collective-permute-start(bf16[8,32,512]{2,1,0:T(8,128)(2,1)S(1)} %get-tuple-element.43), channel_id=1, source_target_pairs={{0,1},{1,0},{2,3},{3,2},{4,5},{5,4},{6,7},{7,6},{8,9},{9,8},{10,11... | collective-permute-start | bytes 786440 | tf_op jit(solution)/shard_map/ppermute | solution.py:346
  49.8 2.9 %collective-permute-start.16 = (bf16[8,32,512]{2,1,0:T(8,128)(2,1)S(1)}, bf16[8,32,512]{2,1,0:T(8,128)(2,1)S(1)}, u32[]{:S(2)}, u32[]{:S(2)}) collective-permute-start(bf16[8,32,512]{2,1,0:T(8,128)(2,1)S(1)} %get-tuple-element.41), channel_id=1, source_target_pairs={{0,16},{1,17},{2,18},{3,19},{4,20},{5,21},{6,22},{7,23},{8,24},{9,... | collective-permute-start | bytes 786440 | tf_op jit(solution)/shard_map/ppermute | solution.py:346
  52.9 0.6 collective-permute-start.4
  53.4 0.8 %collective-permute-done.10 = bf16[8,32,512]{2,1,0:T(8,128)(2,1)S(1)} collective-permute-done((bf16[8,32,512]{2,1,0:T(8,128)(2,1)S(1)}, bf16[8,32,512]{2,1,0:T(8,128)(2,1)S(1)}, u32[]{:S(2)}, u32[]{:S(2)}) %collective-permute-start.10) | collective-permute-done | bytes 262176 | tf_op jit(solution)/shard_map/ppermute | solution.py:346
  54.4 2.9 %collective-permute-start.11 = (bf16[4,32,512]{2,1,0:T(8,128)(2,1)S(1)}, bf16[4,32,512]{2,1,0:T(8,128)(2,1)S(1)}, u32[]{:S(2)}, u32[]{:S(2)}) collective-permute-start(bf16[4,32,512]{2,1,0:T(8,128)(2,1)S(1)} %get-tuple-element.49), channel_id=1, source_target_pairs={{0,3},{1,2},{2,1},{3,0},{4,7},{5,6},{6,5},{7,4},{8,11},{9,10},{10,... | collective-permute-start | bytes 393224 | tf_op jit(solution)/shard_map/ppermute | solution.py:346
  57.4 4.0 %collective-permute-start.17 = (bf16[4,32,512]{2,1,0:T(8,128)(2,1)S(1)}, bf16[4,32,512]{2,1,0:T(8,128)(2,1)S(1)}, u32[]{:S(2)}, u32[]{:S(2)}) collective-permute-start(bf16[4,32,512]{2,1,0:T(8,128)(2,1)S(1)} %get-tuple-element.47), channel_id=1, source_target_pairs={{0,48},{1,49},{2,50},{3,51},{4,52},{5,53},{6,54},{7,55},{8,56},{9,... | collective-permute-start | bytes 393224 | tf_op jit(solution)/shard_map/ppermute | solution.py:346
  61.4 1.1 %collective-permute-start.5 = (bf16[2,32,512]{2,1,0:T(8,128)(2,1)S(1)}, bf16[2,32,512]{2,1,0:T(8,128)(2,1)S(1)}, u32[]{:S(2)}, u32[]{:S(2)}) collective-permute-start(bf16[2,32,512]{2,1,0:T(8,128)(2,1)S(1)} %get-tuple-element.57), channel_id=1, source_target_pairs={{0,1},{1,0},{2,3},{3,2},{4,5},{5,4},{6,7},{7,6},{8,9},{9,8},{10,11... | collective-permute-start | bytes 196616 | tf_op jit(solution)/shard_map/ppermute | solution.py:346
  62.5 2.3 %collective-permute-start.12 = (bf16[2,32,512]{2,1,0:T(8,128)(2,1)S(1)}, bf16[2,32,512]{2,1,0:T(8,128)(2,1)S(1)}, u32[]{:S(2)}, u32[]{:S(2)}) collective-permute-start(bf16[2,32,512]{2,1,0:T(8,128)(2,1)S(1)} %get-tuple-element.55), channel_id=1, source_target_pairs={{0,16},{1,17},{2,18},{3,19},{4,20},{5,21},{6,22},{7,23},{8,24},{9,... | collective-permute-start | bytes 196616 | tf_op jit(solution)/shard_map/ppermute | solution.py:346
  64.9 1.9 %collective-permute-start.18 = (bf16[2,32,512]{2,1,0:T(8,128)(2,1)S(1)}, bf16[2,32,512]{2,1,0:T(8,128)(2,1)S(1)}, u32[]{:S(2)}, u32[]{:S(2)}) collective-permute-start(bf16[2,32,512]{2,1,0:T(8,128)(2,1)S(1)} %get-tuple-element.53), channel_id=1, source_target_pairs={{0,4},{1,5},{2,6},{3,7},{4,0},{5,1},{6,2},{7,3},{8,12},{9,13},{10,... | collective-permute-start | bytes 196616 | tf_op jit(solution)/shard_map/ppermute | solution.py:346
  66.8 3.2 %collective-permute-start.6 = (bf16[1,32,512]{2,1,0:T(8,128)(2,1)S(1)}, bf16[1,32,512]{2,1,0:T(8,128)(2,1)S(1)}, u32[]{:S(2)}, u32[]{:S(2)}) collective-permute-start(bf16[1,32,512]{2,1,0:T(8,128)(2,1)S(1)} %fusion.15), channel_id=1, source_target_pairs={{0,3},{1,2},{2,1},{3,0},{4,7},{5,6},{6,5},{7,4},{8,11},{9,10},{10,... | collective-permute-start | bytes 98312 | tf_op jit(solution)/shard_map/ppermute | solution.py:346
  70.1 3.3 %collective-permute-start.13 = (bf16[1,32,512]{2,1,0:T(8,128)(2,1)S(1)}, bf16[1,32,512]{2,1,0:T(8,128)(2,1)S(1)}, u32[]{:S(2)}, u32[]{:S(2)}) collective-permute-start(bf16[1,32,512]{2,1,0:T(8,128)(2,1)S(1)} %fusion.12), channel_id=1, source_target_pairs={{0,48},{1,49},{2,50},{3,51},{4,52},{5,53},{6,54},{7,55},{8,56},{9,... | collective-permute-start | bytes 98312 | tf_op jit(solution)/shard_map/ppermute | solution.py:346
  73.6 1.7 %collective-permute-done.13 = bf16[1,32,512]{2,1,0:T(8,128)(2,1)S(1)} collective-permute-done((bf16[1,32,512]{2,1,0:T(8,128)(2,1)S(1)}, bf16[1,32,512]{2,1,0:T(8,128)(2,1)S(1)}, u32[]{:S(2)}, u32[]{:S(2)}) %collective-permute-start.13) | collective-permute-done | bytes 32800 | tf_op jit(solution)/shard_map/ppermute | solution.py:346
  75.3 3.3 %collective-permute-done.19 = bf16[1,32,512]{2,1,0:T(8,128)(2,1)S(1)} collective-permute-done((bf16[1,32,512]{2,1,0:T(8,128)(2,1)S(1)}, bf16[1,32,512]{2,1,0:T(8,128)(2,1)S(1)}, u32[]{:S(2)}, u32[]{:S(2)}) %collective-permute-start.19) | collective-permute-done | bytes 32800 | tf_op jit(solution)/shard_map/ppermute | solution.py:346
  78.6 0.6 fusion.22
  (34 shorter events, 2.5 us)
Async XLA Ops:
  5.9 7.2 %collective-permute-start = (bf16[8,512,512]{2,1,0:T(8,128)(2,1)S(1)}, bf16[8,512,512]{2,1,0:T(8,128)(2,1)S(1)}, u32[]{:S(2)}, u32[]{:S(2)}) collective-permute-start(bf16[8,512,512]{2,1,0:T(8,128)(2,1)S(1)} %get-tuple-element.24), channel_id=1, source_target_pairs={{0,64},{64,0},{1,65},{65,1},{2,66},{66,2},{3,67},{67,3},{4,68},{68... | collective-permute-start | bytes 12582920 | tf_op jit(solution)/shard_map/ppermute | solution.py:296
  12.4 5.4 %collective-permute-start.7 = (bf16[5,512,512]{2,1,0:T(8,128)(2,1)S(1)}, bf16[5,512,512]{2,1,0:T(8,128)(2,1)S(1)}, u32[]{:S(2)}, u32[]{:S(2)}) collective-permute-start(bf16[5,512,512]{2,1,0:T(8,128)(2,1)S(1)} %get-tuple-element.28), channel_id=1, source_target_pairs={{0,64},{64,0},{1,65},{65,1},{2,66},{66,2},{3,67},{67,3},{4,68},{68... | collective-permute-start | bytes 7864328 | tf_op jit(solution)/shard_map/ppermute | solution.py:310
  15.8 14.9 %collective-permute-start.1 = (bf16[32,32,512]{2,1,0:T(8,128)(2,1)S(1)}, bf16[32,32,512]{2,1,0:T(8,128)(2,1)S(1)}, u32[]{:S(2)}, u32[]{:S(2)}) collective-permute-start(bf16[32,32,512]{2,1,0:T(8,128)(2,1)S(1)} %get-tuple-element.27), channel_id=1, source_target_pairs={{0,16},{1,17},{2,18},{3,19},{4,20},{5,21},{6,22},{7,23},{8,24},{9,... | collective-permute-start | bytes 3145736 | tf_op jit(solution)/shard_map/ppermute | solution.py:337
  20.4 15.1 %collective-permute-start.8 = (bf16[32,32,512]{2,1,0:T(8,128)(2,1)S(1)}, bf16[32,32,512]{2,1,0:T(8,128)(2,1)S(1)}, u32[]{:S(2)}, u32[]{:S(2)}) collective-permute-start(bf16[32,32,512]{2,1,0:T(8,128)(2,1)S(1)} %get-tuple-element.31), channel_id=1, source_target_pairs={{0,4},{1,5},{2,6},{3,7},{4,0},{5,1},{6,2},{7,3},{8,12},{9,13},{10,... | collective-permute-start | bytes 3145736 | tf_op jit(solution)/shard_map/ppermute | solution.py:337
  23.9 14.9 %collective-permute-start.14 = (bf16[32,32,512]{2,1,0:T(8,128)(2,1)S(1)}, bf16[32,32,512]{2,1,0:T(8,128)(2,1)S(1)}, u32[]{:S(2)}, u32[]{:S(2)}) collective-permute-start(bf16[32,32,512]{2,1,0:T(8,128)(2,1)S(1)} %get-tuple-element.34), channel_id=1, source_target_pairs={{0,1},{1,0},{2,3},{3,2},{4,5},{5,4},{6,7},{7,6},{8,9},{9,8},{10,11... | collective-permute-start | bytes 3145736 | tf_op jit(solution)/shard_map/ppermute | solution.py:337
  31.0 11.3 %collective-permute-start.2 = (bf16[16,32,512]{2,1,0:T(8,128)(2,1)S(1)}, bf16[16,32,512]{2,1,0:T(8,128)(2,1)S(1)}, u32[]{:S(2)}, u32[]{:S(2)}) collective-permute-start(bf16[16,32,512]{2,1,0:T(8,128)(2,1)S(1)} %get-tuple-element.39), channel_id=1, source_target_pairs={{0,48},{1,49},{2,50},{3,51},{4,52},{5,53},{6,54},{7,55},{8,56},{9,... | collective-permute-start | bytes 1572872 | tf_op jit(solution)/shard_map/ppermute | solution.py:346
  35.9 11.8 %collective-permute-start.9 = (bf16[16,32,512]{2,1,0:T(8,128)(2,1)S(1)}, bf16[16,32,512]{2,1,0:T(8,128)(2,1)S(1)}, u32[]{:S(2)}, u32[]{:S(2)}) collective-permute-start(bf16[16,32,512]{2,1,0:T(8,128)(2,1)S(1)} %get-tuple-element.37), channel_id=1, source_target_pairs={{0,12},{1,13},{2,14},{3,15},{4,8},{5,9},{6,10},{7,11},{8,4},{9,5},... | collective-permute-start | bytes 1572872 | tf_op jit(solution)/shard_map/ppermute | solution.py:346
  39.2 10.5 %collective-permute-start.15 = (bf16[16,32,512]{2,1,0:T(8,128)(2,1)S(1)}, bf16[16,32,512]{2,1,0:T(8,128)(2,1)S(1)}, u32[]{:S(2)}, u32[]{:S(2)}) collective-permute-start(bf16[16,32,512]{2,1,0:T(8,128)(2,1)S(1)} %get-tuple-element.35), channel_id=1, source_target_pairs={{0,3},{1,2},{2,1},{3,0},{4,7},{5,6},{6,5},{7,4},{8,11},{9,10},{10,... | collective-permute-start | bytes 1572872 | tf_op jit(solution)/shard_map/ppermute | solution.py:346
  42.5 10.3 %collective-permute-start.3 = (bf16[8,32,512]{2,1,0:T(8,128)(2,1)S(1)}, bf16[8,32,512]{2,1,0:T(8,128)(2,1)S(1)}, u32[]{:S(2)}, u32[]{:S(2)}) collective-permute-start(bf16[8,32,512]{2,1,0:T(8,128)(2,1)S(1)} %get-tuple-element.45), channel_id=1, source_target_pairs={{0,4},{1,5},{2,6},{3,7},{4,0},{5,1},{6,2},{7,3},{8,12},{9,13},{10,... | collective-permute-start | bytes 786440 | tf_op jit(solution)/shard_map/ppermute | solution.py:346
  47.8 6.5 %collective-permute-start.10 = (bf16[8,32,512]{2,1,0:T(8,128)(2,1)S(1)}, bf16[8,32,512]{2,1,0:T(8,128)(2,1)S(1)}, u32[]{:S(2)}, u32[]{:S(2)}) collective-permute-start(bf16[8,32,512]{2,1,0:T(8,128)(2,1)S(1)} %get-tuple-element.43), channel_id=1, source_target_pairs={{0,1},{1,0},{2,3},{3,2},{4,5},{5,4},{6,7},{7,6},{8,9},{9,8},{10,11... | collective-permute-start | bytes 786440 | tf_op jit(solution)/shard_map/ppermute | solution.py:346
  49.8 7.5 %collective-permute-start.16 = (bf16[8,32,512]{2,1,0:T(8,128)(2,1)S(1)}, bf16[8,32,512]{2,1,0:T(8,128)(2,1)S(1)}, u32[]{:S(2)}, u32[]{:S(2)}) collective-permute-start(bf16[8,32,512]{2,1,0:T(8,128)(2,1)S(1)} %get-tuple-element.41), channel_id=1, source_target_pairs={{0,16},{1,17},{2,18},{3,19},{4,20},{5,21},{6,22},{7,23},{8,24},{9,... | collective-permute-start | bytes 786440 | tf_op jit(solution)/shard_map/ppermute | solution.py:346
  52.9 8.5 %collective-permute-start.4 = (bf16[4,32,512]{2,1,0:T(8,128)(2,1)S(1)}, bf16[4,32,512]{2,1,0:T(8,128)(2,1)S(1)}, u32[]{:S(2)}, u32[]{:S(2)}) collective-permute-start(bf16[4,32,512]{2,1,0:T(8,128)(2,1)S(1)} %get-tuple-element.51), channel_id=1, source_target_pairs={{0,12},{1,13},{2,14},{3,15},{4,8},{5,9},{6,10},{7,11},{8,4},{9,5},... | collective-permute-start | bytes 393224 | tf_op jit(solution)/shard_map/ppermute | solution.py:346
  54.4 8.1 %collective-permute-start.11 = (bf16[4,32,512]{2,1,0:T(8,128)(2,1)S(1)}, bf16[4,32,512]{2,1,0:T(8,128)(2,1)S(1)}, u32[]{:S(2)}, u32[]{:S(2)}) collective-permute-start(bf16[4,32,512]{2,1,0:T(8,128)(2,1)S(1)} %get-tuple-element.49), channel_id=1, source_target_pairs={{0,3},{1,2},{2,1},{3,0},{4,7},{5,6},{6,5},{7,4},{8,11},{9,10},{10,... | collective-permute-start | bytes 393224 | tf_op jit(solution)/shard_map/ppermute | solution.py:346
  57.4 7.5 %collective-permute-start.17 = (bf16[4,32,512]{2,1,0:T(8,128)(2,1)S(1)}, bf16[4,32,512]{2,1,0:T(8,128)(2,1)S(1)}, u32[]{:S(2)}, u32[]{:S(2)}) collective-permute-start(bf16[4,32,512]{2,1,0:T(8,128)(2,1)S(1)} %get-tuple-element.47), channel_id=1, source_target_pairs={{0,48},{1,49},{2,50},{3,51},{4,52},{5,53},{6,54},{7,55},{8,56},{9,... | collective-permute-start | bytes 393224 | tf_op jit(solution)/shard_map/ppermute | solution.py:346
  61.4 5.5 %collective-permute-start.5 = (bf16[2,32,512]{2,1,0:T(8,128)(2,1)S(1)}, bf16[2,32,512]{2,1,0:T(8,128)(2,1)S(1)}, u32[]{:S(2)}, u32[]{:S(2)}) collective-permute-start(bf16[2,32,512]{2,1,0:T(8,128)(2,1)S(1)} %get-tuple-element.57), channel_id=1, source_target_pairs={{0,1},{1,0},{2,3},{3,2},{4,5},{5,4},{6,7},{7,6},{8,9},{9,8},{10,11... | collective-permute-start | bytes 196616 | tf_op jit(solution)/shard_map/ppermute | solution.py:346
  62.5 7.6 %collective-permute-start.12 = (bf16[2,32,512]{2,1,0:T(8,128)(2,1)S(1)}, bf16[2,32,512]{2,1,0:T(8,128)(2,1)S(1)}, u32[]{:S(2)}, u32[]{:S(2)}) collective-permute-start(bf16[2,32,512]{2,1,0:T(8,128)(2,1)S(1)} %get-tuple-element.55), channel_id=1, source_target_pairs={{0,16},{1,17},{2,18},{3,19},{4,20},{5,21},{6,22},{7,23},{8,24},{9,... | collective-permute-start | bytes 196616 | tf_op jit(solution)/shard_map/ppermute | solution.py:346
  64.9 8.5 %collective-permute-start.18 = (bf16[2,32,512]{2,1,0:T(8,128)(2,1)S(1)}, bf16[2,32,512]{2,1,0:T(8,128)(2,1)S(1)}, u32[]{:S(2)}, u32[]{:S(2)}) collective-permute-start(bf16[2,32,512]{2,1,0:T(8,128)(2,1)S(1)} %get-tuple-element.53), channel_id=1, source_target_pairs={{0,4},{1,5},{2,6},{3,7},{4,0},{5,1},{6,2},{7,3},{8,12},{9,13},{10,... | collective-permute-start | bytes 196616 | tf_op jit(solution)/shard_map/ppermute | solution.py:346
  66.8 6.7 %collective-permute-start.6 = (bf16[1,32,512]{2,1,0:T(8,128)(2,1)S(1)}, bf16[1,32,512]{2,1,0:T(8,128)(2,1)S(1)}, u32[]{:S(2)}, u32[]{:S(2)}) collective-permute-start(bf16[1,32,512]{2,1,0:T(8,128)(2,1)S(1)} %fusion.15), channel_id=1, source_target_pairs={{0,3},{1,2},{2,1},{3,0},{4,7},{5,6},{6,5},{7,4},{8,11},{9,10},{10,... | collective-permute-start | bytes 98312 | tf_op jit(solution)/shard_map/ppermute | solution.py:346
  70.1 5.2 %collective-permute-start.13 = (bf16[1,32,512]{2,1,0:T(8,128)(2,1)S(1)}, bf16[1,32,512]{2,1,0:T(8,128)(2,1)S(1)}, u32[]{:S(2)}, u32[]{:S(2)}) collective-permute-start(bf16[1,32,512]{2,1,0:T(8,128)(2,1)S(1)} %fusion.12), channel_id=1, source_target_pairs={{0,48},{1,49},{2,50},{3,51},{4,52},{5,53},{6,54},{7,55},{8,56},{9,... | collective-permute-start | bytes 98312 | tf_op jit(solution)/shard_map/ppermute | solution.py:346
  73.4 5.2 %collective-permute-start.19 = (bf16[1,32,512]{2,1,0:T(8,128)(2,1)S(1)}, bf16[1,32,512]{2,1,0:T(8,128)(2,1)S(1)}, u32[]{:S(2)}, u32[]{:S(2)}) collective-permute-start(bf16[1,32,512]{2,1,0:T(8,128)(2,1)S(1)} %fusion.9), channel_id=1, source_target_pairs={{0,12},{1,13},{2,14},{3,15},{4,8},{5,9},{6,10},{7,11},{8,4},{9,5},... | collective-permute-start | bytes 98312 | tf_op jit(solution)/shard_map/ppermute | solution.py:346
  75.3 3.3 %copy-start = (bf16[12,8,512]{2,1,0:T(8,128)(2,1)}, bf16[12,8,512]{2,1,0:T(8,128)(2,1)S(1)}, u32[]{:S(2)}) copy-start(bf16[12,8,512]{2,1,0:T(8,128)(2,1)S(1)} %fusion.20) | copy-start | bytes 294916
